TPU v7x, 32 devices: a whole 2x2x4 slice. The times are simulated.
32 devices in a mesh: heads: 2 (over core), seq: 16 (over z, y, x).
Axes of the slice: x: 2, y: 2, z: 4, core: 2. Of those that a mesh axis runs over, the one named last changes fastest.
Arguments:
- tokens: bfloat16 [16384, 768], P('seq'), may hold values from -6 to 6
- gain_attn: bfloat16 [768], replicated, may hold values from 0.5 to 1.5
- w_query: bfloat16 [768, 768], P(None, 'heads'), may hold values from -0.21875 to 0.21875
- w_key: bfloat16 [768, 768], P(None, 'heads'), may hold values from -0.21875 to 0.21875
- w_value: bfloat16 [768, 768], P(None, 'heads'), may hold values from -0.21875 to 0.21875
- w_out: bfloat16 [768, 768], P('heads'), may hold values from -1.25 to 1.25
- bias_table: bfloat16 [32, 12], P(None, 'heads'), may hold values from -4 to 4
- gain_ffn: bfloat16 [768], replicated, may hold values from 0.5 to 1.5
- w_router: bfloat16 [768, 16], replicated, may hold values from -0.21875 to 0.21875
- w_inner: bfloat16 [16, 768, 3072], P('seq', None, 'heads'), may hold values from -0.21875 to 0.21875
- w_outer: bfloat16 [16, 3072, 768], P('seq', 'heads'), may hold values from -6 to 6
- routes: int32 [16384, 1], P('seq'), may hold values from 0 to 15
- seq_lengths: int32 [80], P('seq'), may hold values from 64 to 512, as said below
- out_grad: bfloat16 [16384, 768], P('seq'), may hold values from -6 to 6
Outputs:
- out: bfloat16 [16384, 768], P('seq', 'heads')
- input_grad: float32 [16384, 768], P('seq')
- gain_attn_grad: float32 [768], replicated
- query_w_grad: float32 [768, 768], P(None, 'heads')
- key_w_grad: float32 [768, 768], P(None, 'heads')
- value_w_grad: float32 [768, 768], P(None, 'heads')
- out_w_grad: float32 [768, 768], P('heads')
- table_grad: float32 [32, 12], P(None, 'heads')
- gain_ffn_grad: float32 [768], replicated
- router_grad: float32 [768, 16], replicated
- inner_grad: float32 [16, 768, 3072], P('seq', None, 'heads')
- outer_grad: float32 [16, 3072, 768], P('seq', 'heads')
Inputs may be any that keep to these rules, and one draw needn't show every extreme that they name: `seq_lengths`: sequence k of an index of seq: the first 4 come from the bucket of 128 slots and hold at least 64 tokens, the other 1 from the bucket of 512 slots and hold at least 256; on every index of seq one of them fills its bucket.
All inputs are finite; a program needn't handle non-finite values.
Results may differ from a plain program's by a relative error of at most 0.017.
Values may be sent and summed in bfloat16 or wider, within the bound.
No kernel may reach another device: no remote copies, remote signals or barrier semaphores. Data moves between devices by JAX's collectives and lax.ppermute only.
A program may use at most 128 MiB of HBM per device.

v0:
```python
from functools import partial

import jax
import jax.numpy as jnp
from jax import lax
from jax.experimental import pallas as pl
from jax.experimental.pallas import tpu as pltpu
from jax.sharding import PartitionSpec as P

SHORT_LEN = 128
LONG_LEN = 512
SHORT_DEV = 4
LONG_DEV = 1


epsilon = 1e-06
highest = lax.Precision.HIGHEST
far_limits = (12, 16, 23, 32, 46, 64, 91)


def vmem(count):
    return [pl.BlockSpec(memory_space=pltpu.VMEM)] * count


def params(mib=16):
    return pltpu.CompilerParams(vmem_limit_bytes=mib * 1024 * 1024)


def dot_nn(left, right):
    return jnp.dot(left, right, preferred_element_type=jnp.float32)


def dot_nt(left, right):
    return lax.dot_general(
        left, right, (((1,), (1,)), ((), ())), preferred_element_type=jnp.float32
    )


def inverse_rms(values):
    return lax.rsqrt(jnp.mean(values * values, axis=-1, keepdims=True) + epsilon)


def diagonal_buckets(offset):
    distance = jnp.abs(offset)
    far_bucket = jnp.full(offset.shape, 8, jnp.int32)
    for limit in far_limits:
        far_bucket = far_bucket + (distance >= limit).astype(jnp.int32)
    return jnp.where(distance < 8, distance, far_bucket) + jnp.where(offset > 0, 16, 0)


def hbm_out(shape, dtype):
    return pltpu.HBM(shape, dtype)


def in_hbm(array):
    return pltpu.with_memory_space_constraint(array, pltpu.HBM)


def start_copies(pairs):
    copies = [pltpu.make_async_copy(*triple) for triple in pairs]
    for copy in copies:
        copy.start()
    return copies


def attend_kernel(
    block_rows,
    lengths_ref,
    tokens_hbm,
    gain_ref,
    wq_hbm,
    wk_hbm,
    wv_hbm,
    wo_hbm,
    table_ref,
    part_hbm,
    normed_hbm,
    q_hbm,
    k_hbm,
    v_hbm,
    mixed_hbm,
    long_hbm,
    short_hbm,
    tokens_ref,
    joint_ref,
    wo_ref,
    part_ref,
    normed_ref,
    q_ref,
    k_ref,
    v_ref,
    mixed_ref,
    long_ref,
    short_ref,
    diag_ref,
    in_sems,
    out_sems,
):
    tok_count, width = tokens_ref.shape
    own = q_ref.shape[1]
    pairs = own // 128
    short_tok = SHORT_DEV * SHORT_LEN
    tile = 512
    steps = tok_count // tile
    tiles_in = []
    for step in range(steps):
        rows = slice(step * tile, step * tile + tile)
        tiles_in.append((tokens_hbm.at[rows], tokens_ref.at[rows], in_sems.at[step]))
    weights = [
        (source, joint_ref.at[:, index * own : index * own + own])
        for index, source in enumerate((wq_hbm, wk_hbm, wv_hbm))
    ]
    weights.append((wo_hbm, wo_ref))
    copies = start_copies(
        tiles_in + [(src, dst, in_sems.at[steps + index]) for index, (src, dst) in enumerate(weights)]
    )
    weight_copies = copies[steps:]
    outs = []

    offset = lax.broadcasted_iota(jnp.int32, (table_ref.shape[1], 512), 1) - 256
    hot = jnp.where(
        diagonal_buckets(offset)
        == lax.broadcasted_iota(jnp.int32, (table_ref.shape[1], 512), 0),
        1.0,
        0.0,
    )
    diag_ref[...] = dot_nn(table_ref[...], hot.astype(jnp.bfloat16))
    gain = gain_ref[...]

    def normalize(step, carry):
        rows = pl.ds(pl.multiple_of(step * tile, tile), tile)
        pltpu.make_async_copy(tokens_hbm.at[rows], tokens_ref.at[rows], in_sems.at[step]).wait()
        values = tokens_ref[rows, :].astype(jnp.float32)
        normed_ref[rows, :] = (values * inverse_rms(values) * gain).astype(jnp.bfloat16)
        return carry

    lax.fori_loop(0, steps, normalize, 0)
    outs += start_copies([(normed_ref, normed_hbm, out_sems.at[0])])
    for copy in weight_copies[:3]:
        copy.wait()

    def project(step, carry):
        rows = pl.ds(pl.multiple_of(step * tile, tile), tile)
        joint = dot_nn(normed_ref[rows, :], joint_ref[...]).astype(jnp.bfloat16)
        q_ref[rows, :] = joint[:, :own] * jnp.bfloat16(0.125)
        k_ref[rows, :] = joint[:, own : 2 * own]
        v_ref[rows, :] = joint[:, 2 * own :]
        return carry

    lax.fori_loop(0, steps, project, 0)
    outs += start_copies(
        [
            (q_ref, q_hbm, out_sems.at[1]),
            (k_ref, k_hbm, out_sems.at[2]),
            (v_ref, v_hbm, out_sems.at[3]),
        ]
    )
    lane = lax.broadcasted_iota(jnp.int32, (1, 128), 1)
    key_place = lax.broadcasted_iota(jnp.int32, (1, LONG_LEN), 1)
    live_long = key_place < lengths_ref[SHORT_DEV]

    def softmax(scores):
        weights = jnp.exp(scores - jnp.max(scores, axis=1, keepdims=True))
        return (weights * (1.0 / jnp.sum(weights, axis=1, keepdims=True))).astype(jnp.bfloat16)

    def one_pair(pair):
        lanes = slice(pair * 128, pair * 128 + 128)
        tiles = []
        for sub in range(2):
            row = diag_ref[pair * 2 + sub : pair * 2 + sub + 1, :]
            spread = pltpu.roll(
                jnp.broadcast_to(row, (128, 512)), 256, 1, stride=1, stride_axis=0
            )
            tiles.append(
                (
                    spread[:, 0:128],
                    spread[:, 128:256],
                    spread[:, 384:512],
                    jnp.broadcast_to(row[:, 511:512], (128, 128)),
                    jnp.broadcast_to(row[:, 0:1], (128, 128)),
                )
            )
        out = []
        for sub in range(2):
            scores = []
            for block in range(SHORT_DEV):
                rows = slice(block * 128, block * 128 + 128)
                masked = jnp.where((lane >= 64) == (sub == 1), q_ref[rows, lanes], 0)
                live = key_place[:, :128] < lengths_ref[block]
                scores.append(
                    jnp.where(
                        live, dot_nt(masked, k_ref[rows, lanes]) + tiles[sub][0], -1000000000.0
                    )
                )
            probs = softmax(jnp.concatenate(scores, axis=0))
            short_ref[pair * 2 + sub] = probs
            mixed = []
            for block in range(SHORT_DEV):
                rows = slice(block * 128, block * 128 + 128)
                mixed.append(dot_nn(probs[rows], v_ref[rows, lanes]))
            out.append(jnp.concatenate(mixed, axis=0))
        mixed_ref[:short_tok, lanes] = jnp.where(lane < 64, out[0], out[1]).astype(jnp.bfloat16)
        keys = k_ref[short_tok:, lanes]
        values = v_ref[short_tok:, lanes]
        for start in range(0, LONG_LEN, block_rows):
            places = slice(start, start + block_rows)
            rows = slice(short_tok + start, short_tok + start + block_rows)
            queries = q_ref[rows, lanes]
            out = []
            for sub in range(2):
                masked = jnp.where((lane >= 64) == (sub == 1), queries, 0)
                same, above, below, far_above, far_below = tiles[sub]
                bias = jnp.concatenate(
                    [
                        jnp.concatenate(
                            [
                                same
                                if other == block
                                else above
                                if other == block + 1
                                else below
                                if other == block - 1
                                else far_above
                                if other > block
                                else far_below
                                for other in range(LONG_LEN // 128)
                            ],
                            axis=1,
                        )
                        for block in range(start // 128, (start + block_rows) // 128)
                    ],
                    axis=0,
                )
                scores = jnp.where(live_long, dot_nt(masked, keys) + bias, -1000000000.0)
                probs = softmax(scores)
                long_ref[pair * 2 + sub, places, :] = probs
                out.append(dot_nn(probs, values))
            mixed_ref[rows, lanes] = jnp.where(lane < 64, out[0], out[1]).astype(jnp.bfloat16)

    for pair in range(pairs):
        one_pair(pair)
        both = slice(pair * 2, pair * 2 + 2)
        outs += start_copies(
            [
                (long_ref.at[both], long_hbm.at[both], out_sems.at[4 + 2 * pair]),
                (short_ref.at[both], short_hbm.at[both], out_sems.at[5 + 2 * pair]),
            ]
        )
    weight_copies[3].wait()
    base = 4 + 2 * pairs
    outs += start_copies([(mixed_ref, mixed_hbm, out_sems.at[base])])

    def part_copy(step):
        rows = pl.ds(pl.multiple_of(step * tile, tile), tile)
        return pltpu.make_async_copy(part_ref.at[rows], part_hbm.at[rows], out_sems.at[base + 1 + step])

    def project_out(step, carry):
        rows = pl.ds(pl.multiple_of(step * tile, tile), tile)
        part_ref[rows, :] = dot_nn(mixed_ref[rows, :], wo_ref[...]).astype(part_ref.dtype)
        part_copy(step).start()
        return carry

    lax.fori_loop(0, steps, project_out, 0)
    outs += [part_copy(step) for step in range(steps)]
    for copy in outs:
        copy.wait()


def attend(lengths, tokens, gain, w_query, w_key, w_value, w_out, table, block_rows=512):
    tok_count, width = tokens.shape
    own = w_query.shape[1]
    heads = own // 64
    heads_pad = -(-heads // 8) * 8
    table = jnp.pad(table.T, ((0, heads_pad - heads), (0, 0)))
    short_tok = SHORT_DEV * SHORT_LEN
    flops = 2 * tok_count * width * own * 4 + 4 * heads * (512 * 512 + short_tok * 128) * 64
    hbm = pl.BlockSpec(memory_space=pltpu.HBM)
    out_shapes = [
        ((tok_count, width), jnp.bfloat16),
        ((tok_count, width), jnp.bfloat16),
        ((tok_count, own), jnp.bfloat16),
        ((tok_count, own), jnp.bfloat16),
        ((tok_count, own), jnp.bfloat16),
        ((tok_count, own), jnp.bfloat16),
        ((heads, LONG_LEN, LONG_LEN), jnp.bfloat16),
        ((heads, short_tok, SHORT_LEN), jnp.bfloat16),
    ]
    steps = tok_count // 512
    return pl.pallas_call(
        partial(attend_kernel, block_rows),
        out_shape=[jax.ShapeDtypeStruct(*out_shapes[0])]
        + [hbm_out(shape, dtype) for shape, dtype in out_shapes[1:]],
        in_specs=[pl.BlockSpec(memory_space=pltpu.SMEM), hbm]
        + vmem(1)
        + [hbm] * 4
        + vmem(1),
        out_specs=[hbm] * 8,
        scratch_shapes=[pltpu.VMEM(tokens.shape, jnp.bfloat16)]
        + [pltpu.VMEM((width, 3 * own), jnp.bfloat16), pltpu.VMEM(w_out.shape, jnp.bfloat16)]
        + [pltpu.VMEM(shape, dtype) for shape, dtype in out_shapes]
        + [
            pltpu.VMEM((heads_pad, 512), jnp.float32),
            pltpu.SemaphoreType.DMA((steps + 4,)),
            pltpu.SemaphoreType.DMA((5 + 2 * (heads // 2) + steps,)),
        ],
        compiler_params=params(24),
        cost_estimate=pl.CostEstimate(
            flops=flops, bytes_accessed=16000000, transcendentals=heads * 512 * 640
        ),
        name="attend",
    )(
        lengths,
        in_hbm(tokens),
        gain.astype(jnp.float32)[None],
        in_hbm(w_query),
        in_hbm(w_key),
        in_hbm(w_value),
        in_hbm(w_out),
        table,
    )


def score_part(probs, prob_grad):
    mean = jnp.sum(probs * prob_grad, axis=1, keepdims=True) / jnp.sum(probs, axis=1, keepdims=True)
    return probs * (prob_grad - mean)


def attend_back_pair(
    pair, hg_ref, q_ref, k_ref, v_ref, long_ref, short_ref, grads_ref, tiles_ref, far_ref, sg_ref,
):
    short_tok = SHORT_DEV * SHORT_LEN
    lane = lax.broadcasted_iota(jnp.int32, (1, 128), 1)
    lanes = pl.ds(pl.multiple_of(pair * 128, 128), 128)
    blocks = LONG_LEN // 128
    heads_grad = hg_ref[:, lanes]
    q_t = jnp.transpose(q_ref[:, lanes])
    hg_t = jnp.transpose(heads_grad)
    qg = []
    kg_t = []
    vg_t = []
    for sub in range(2):
        head = pair * 2 + sub
        own = (lane >= 64) == (sub == 1)
        rows_t = slice(64 * sub, 64 * sub + 64)
        masked = jnp.where(own, heads_grad, 0)
        grads = [
            dot_nt(masked[block * 128 : block * 128 + 128], v_ref[block * 128 : block * 128 + 128, lanes])
            for block in range(SHORT_DEV)
        ]
        probs = short_ref[head]
        part = score_part(probs.astype(jnp.float32), jnp.concatenate(grads, axis=0))
        same = part[:128]
        for block in range(1, SHORT_DEV):
            same = same + part[block * 128 : block * 128 + 128]
        part = part.astype(jnp.bfloat16)
        qg_parts = []
        kg_parts = []
        vg_parts = []
        for block in range(SHORT_DEV):
            rows = slice(block * 128, block * 128 + 128)
            qg_parts.append(dot_nn(part[rows], k_ref[rows, lanes]))
            kg_parts.append(dot_nn(q_t[rows_t, rows], part[rows]))
            vg_parts.append(dot_nn(hg_t[rows_t, rows], probs[rows]))
        above = jnp.zeros((128, 128), jnp.float32)
        below = above
        far_above = above
        far_below = above
        probs = long_ref[head]
        part = score_part(
            probs.astype(jnp.float32), dot_nt(masked[short_tok:], v_ref[short_tok:, lanes])
        )
        for block in range(blocks):
            for other in range(blocks):
                piece = part[block * 128 : block * 128 + 128, other * 128 : other * 128 + 128]
                if other == block:
                    same = same + piece
                elif other == block + 1:
                    above = above + piece
                elif other == block - 1:
                    below = below + piece
                elif other > block:
                    far_above = far_above + piece
                else:
                    far_below = far_below + piece
        sg_ref[...] = part.astype(jnp.bfloat16)
        qg_parts.append(dot_nn(sg_ref[...], k_ref[short_tok:, lanes]))
        kg_parts.append(dot_nn(q_t[rows_t, short_tok:], sg_ref[...]))
        vg_parts.append(dot_nn(hg_t[rows_t, short_tok:], probs))
        qg.append(jnp.concatenate(qg_parts, axis=0))
        kg_t.append(jnp.concatenate(kg_parts, axis=1))
        vg_t.append(jnp.concatenate(vg_parts, axis=1))
        tiles_ref[head, :, 0:128] = same
        tiles_ref[head, :, 128:256] = above
        tiles_ref[head, :, 256:384] = below
        far_ref[head, 0:1, :] = jnp.sum(far_above, axis=0, keepdims=True)
        far_ref[head, 1:2, :] = jnp.sum(far_below, axis=0, keepdims=True)
    width = q_ref.shape[1]
    grads_ref[:, lanes] = (jnp.where(lane < 64, qg[0], qg[1]) * 0.125).astype(jnp.bfloat16)
    for index, whole in ((1, kg_t), (2, vg_t)):
        place = pl.ds(pl.multiple_of(index * width + pair * 128, 128), 128)
        grads_ref[:, place] = jnp.transpose(jnp.concatenate(whole, axis=0).astype(jnp.bfloat16))


def diagonals(tiles):
    tile = jnp.concatenate(
        [tiles[:, 0:256], jnp.zeros((128, 128), jnp.float32), tiles[:, 256:384]], axis=1
    )
    span = 64
    while span:
        tile = tile[:span] + pltpu.roll(tile[span:], 512 - span, 1)
        span //= 2
    return tile


def table_from(diag, bucket_count):
    lane = jnp.arange(768, dtype=jnp.int32)
    offset = jnp.where(lane < 256, lane, lane - 512)
    offset = jnp.where(lane >= 640, -256, jnp.where(lane >= 512, 256, offset))
    hot = (diagonal_buckets(offset)[:, None] == jnp.arange(bucket_count)[None, :]).astype(jnp.float32)
    return lax.dot_general(
        hot, diag, (((0,), (1,)), ((), ())), precision=highest, preferred_element_type=jnp.float32
    )


def dispatch_rows(send_ref, slot_row, half_rows):
    slots = send_ref.shape[0]
    tok_count = slot_row.shape[1]
    span = slots
    for base in range(0, slots, span):
        place = lax.broadcasted_iota(jnp.int32, (span, tok_count), 0) + base
        hot = jnp.where(place == slot_row, 1.0, 0.0).astype(jnp.bfloat16)
        send_ref[base : base + span, :] = dot_nn(hot, half_rows).astype(jnp.bfloat16)


def half_lanes(core, half):
    return pl.ds(pl.multiple_of(core * half, half), half)


def route_kernel(
    capacity, where_ref, routes_hbm, grad_hbm, row_hbm, send_ref, routes_ref, grad_ref, row_ref, in_sems,
    out_sem,
):
    tok_count = routes_ref.shape[1]
    slots, half = send_ref.shape
    experts = slots // capacity
    fetch, copy = start_copies(
        [
            (routes_hbm, routes_ref, in_sems.at[0]),
            (grad_hbm.at[:, half_lanes(where_ref[0], half)], grad_ref, in_sems.at[1]),
        ]
    )
    fetch.wait()
    routes = routes_ref[...]
    expert = lax.broadcasted_iota(jnp.int32, (experts, tok_count), 0)
    lane = lax.broadcasted_iota(jnp.int32, (1, tok_count), 1)
    hot = jnp.where(expert == routes, 1.0, 0.0)
    total = hot
    step = 1
    while step < tok_count:
        total = total + jnp.where(lane >= step, pltpu.roll(total, step, 1), 0.0)
        step *= 2
    before = jnp.sum(hot * total, axis=0, keepdims=True).astype(jnp.int32) - 1
    slot = jnp.where(before < capacity, routes * capacity + before, slots)
    row_ref[...] = slot
    out = pltpu.make_async_copy(row_ref, row_hbm, out_sem)
    out.start()
    copy.wait()
    dispatch_rows(send_ref, slot, grad_ref[...])
    out.wait()


def route(where, routes, out_grad, experts, capacity):
    tok_count, width = out_grad.shape
    slots = experts * capacity
    return pl.pallas_call(
        partial(route_kernel, capacity),
        out_shape=[
            hbm_out((1, tok_count), jnp.int32),
            jax.ShapeDtypeStruct((slots, width // 2), jnp.bfloat16),
        ],
        in_specs=[
            pl.BlockSpec(memory_space=pltpu.SMEM),
            pl.BlockSpec(memory_space=pltpu.HBM),
            pl.BlockSpec(memory_space=pltpu.HBM),
        ],
        out_specs=[pl.BlockSpec(memory_space=pltpu.HBM)] + vmem(1),
        scratch_shapes=[
            pltpu.VMEM((1, tok_count), jnp.int32),
            pltpu.VMEM((tok_count, width // 2), jnp.bfloat16),
            pltpu.VMEM((1, tok_count), jnp.int32),
            pltpu.SemaphoreType.DMA((2,)),
            pltpu.SemaphoreType.DMA,
        ],
        compiler_params=params(28),
        cost_estimate=pl.CostEstimate(
            flops=slots * tok_count * width, bytes_accessed=4000000, transcendentals=0
        ),
        name="route",
    )(where, in_hbm(routes.reshape(1, tok_count)), in_hbm(out_grad))


def second_kernel(
    where_ref, tokens_hbm, own_ref, other_ref, gain_ref, row_hbm, residual_hbm, send_ref, tokens_ref,
    row_ref, residual_ref, second_ref, in_sems, out_sems,
):
    tile = 256
    tok_count = tokens_ref.shape[0]
    half = send_ref.shape[1]
    tiles_rows = [slice(start, start + tile) for start in range(0, tok_count, tile)]
    copies = start_copies(
        [
            (tokens_hbm.at[rows], tokens_ref.at[rows], in_sems.at[step])
            for step, rows in enumerate(tiles_rows)
        ]
        + [(row_hbm, row_ref, in_sems.at[len(tiles_rows)])]
    )
    outs = []
    gain = gain_ref[...]
    for step, rows in enumerate(tiles_rows):
        attn = own_ref[rows, :].astype(jnp.float32) + other_ref[rows, :].astype(jnp.float32)
        copies[step].wait()
        residual = tokens_ref[rows, :].astype(jnp.float32) + attn
        residual_ref[rows, :] = residual
        outs += start_copies([(residual_ref.at[rows], residual_hbm.at[rows], out_sems.at[step])])
        second_ref[rows, :] = (residual * inverse_rms(residual) * gain).astype(jnp.bfloat16)
    copies[-1].wait()
    dispatch_rows(send_ref, row_ref[...], second_ref[:, half_lanes(where_ref[0], half)])
    for copy in outs:
        copy.wait()


def second_rows(where, tokens, own, other, gain, slot_row, slots):
    tok_count, width = tokens.shape
    steps = tok_count // 256
    hbm = pl.BlockSpec(memory_space=pltpu.HBM)
    return pl.pallas_call(
        second_kernel,
        out_shape=[
            hbm_out((tok_count, width), jnp.float32),
            jax.ShapeDtypeStruct((slots, width // 2), jnp.bfloat16),
        ],
        in_specs=[pl.BlockSpec(memory_space=pltpu.SMEM), hbm] + vmem(3) + [hbm],
        out_specs=[hbm] + vmem(1),
        scratch_shapes=[
            pltpu.VMEM((tok_count, width), jnp.bfloat16),
            pltpu.VMEM((1, tok_count), jnp.int32),
            pltpu.VMEM((tok_count, width), jnp.float32),
            pltpu.VMEM((tok_count, width), jnp.bfloat16),
            pltpu.SemaphoreType.DMA((steps + 1,)),
            pltpu.SemaphoreType.DMA((steps,)),
        ],
        compiler_params=params(28),
        cost_estimate=pl.CostEstimate(
            flops=slots * tok_count * width, bytes_accessed=13000000, transcendentals=0
        ),
        name="second",
    )(where, in_hbm(tokens), own, other, gain.astype(jnp.float32)[None], in_hbm(slot_row))


def hidden_grad_kernel(where_ref, own_ref, other_ref, outer_ref, out_ref, whole_ref):
    half = own_ref.shape[1]
    core = where_ref[0]
    whole_ref[:, half_lanes(core, half)] = own_ref[...]
    whole_ref[:, half_lanes(1 - core, half)] = other_ref[...]
    out_ref[...] = dot_nt(whole_ref[...], outer_ref[...]).astype(jnp.bfloat16)


def hidden_grad_of(where, own, other, outer):
    slots, half = own.shape
    hidden = outer.shape[0]
    tile = 256
    rows = pl.BlockSpec((tile, half), lambda step: (step, 0))
    return pl.pallas_call(
        hidden_grad_kernel,
        grid=(slots // tile,),
        out_shape=hbm_out((slots, hidden), jnp.bfloat16),
        in_specs=[pl.BlockSpec(memory_space=pltpu.SMEM), rows, rows] + vmem(1),
        out_specs=pl.BlockSpec((tile, hidden), lambda step: (step, 0)),
        scratch_shapes=[pltpu.VMEM((tile, 2 * half), jnp.bfloat16)],
        compiler_params=params(),
        cost_estimate=pl.CostEstimate(
            flops=4 * slots * half * hidden, bytes_accessed=12000000, transcendentals=0
        ),
        name="hidden_grad",
    )(where, own, other, outer)


def gate_of(rows, router, index):
    experts = router.shape[1]
    logits = dot_nn(rows, router)
    exp_logit = jnp.exp(logits - jnp.max(logits, axis=1, keepdims=True))
    probs = exp_logit * (1.0 / jnp.sum(exp_logit, axis=1, keepdims=True))
    hit = jnp.where(lax.broadcasted_iota(jnp.int32, (1, experts), 1) == index, 1.0, 0.0)
    return probs, hit, jnp.sum(probs * hit, axis=1, keepdims=True)


def expert_kernel(
    where_ref,
    own_ref,
    other_ref,
    hg_ref,
    inner_ref,
    router_ref,
    hidden_ref,
    pre_grad_ref,
    keep_ref,
    send_ref,
    logit_ref,
    arrived_ref,
    whole_ref,
):
    core = where_ref[0]
    tile, half = own_ref.shape
    own_lanes = half_lanes(core, half)
    other_lanes = half_lanes(1 - core, half)
    arrived_ref[:, own_lanes] = own_ref[...]
    arrived_ref[:, other_lanes] = other_ref[...]
    arrived = arrived_ref[...]
    probs, hit, gate = gate_of(arrived, router_ref[...], where_ref[1])
    curve = 0.7978845608028654
    gate_grad = jnp.zeros((tile, 1), jnp.float32)
    back = jnp.zeros((tile, 2 * half), jnp.float32)
    chunk = 512
    for start in range(0, hg_ref.shape[1], chunk):
        cols = slice(start, start + chunk)
        pre = dot_nn(arrived, inner_ref[:, cols])
        square = pre * pre
        share = 0.5 + 0.5 * jnp.tanh(pre * (curve + (curve * 0.044715) * square))
        hidden_ref[:, cols] = (pre * share).astype(jnp.bfloat16)
        passed = share * hg_ref[:, cols].astype(jnp.float32)
        gate_grad = gate_grad + jnp.sum(pre * passed, axis=1, keepdims=True)
        bend = pre * (2.0 * curve + (6.0 * curve * 0.044715) * square)
        pre_grad = ((gate * passed) * (1.0 + (1.0 - share) * bend)).astype(jnp.bfloat16)
        pre_grad_ref[:, cols] = pre_grad
        back = back + dot_nt(pre_grad, inner_ref[:, cols])
    logit = (probs * (gate_grad * (hit - gate))).astype(jnp.bfloat16)
    logit_ref[...] = logit
    whole_ref[...] = back + dot_nt(logit, router_ref[...])
    send_ref[...] = whole_ref[:, other_lanes].astype(jnp.bfloat16)
    keep_ref[...] = whole_ref[:, own_lanes]


def expert(where, own, other, hidden_grad, inner, router):
    slots, half = own.shape
    width, hidden = inner.shape
    experts = router.shape[1]
    tile = 256
    halves = pl.BlockSpec((tile, half), lambda step: (step, 0))
    units = pl.BlockSpec((tile, hidden), lambda step: (step, 0))
    return pl.pallas_call(
        expert_kernel,
        grid=(slots // tile,),
        out_shape=[
            hbm_out((slots, hidden), jnp.bfloat16),
            hbm_out((slots, hidden), jnp.bfloat16),
            jax.ShapeDtypeStruct((slots, half), jnp.float32),
            jax.ShapeDtypeStruct((slots, half), jnp.bfloat16),
            hbm_out((slots, experts), jnp.bfloat16),
        ],
        in_specs=[
            pl.BlockSpec(memory_space=pltpu.SMEM),
            halves,
            halves,
            units,
            pl.BlockSpec(inner.shape, lambda step: (0, 0), pipeline_mode=pl.Buffered(1)),
        ]
        + vmem(1),
        out_specs=[
            units,
            units,
            halves,
            halves,
            pl.BlockSpec((tile, experts), lambda step: (step, 0)),
        ],
        scratch_shapes=[
            pltpu.VMEM((tile, width), jnp.bfloat16),
            pltpu.VMEM((tile, width), jnp.float32),
        ],
        compiler_params=params(),
        cost_estimate=pl.CostEstimate(
            flops=4 * slots * width * hidden, bytes_accessed=20000000, transcendentals=slots * hidden
        ),
        name="expert",
    )(where, own, other, in_hbm(hidden_grad), in_hbm(inner), router)


def expert_out_kernel(
    where_ref, hidden_ref, own_ref, other_ref, logit_ref, row_ref, outer_ref, keep_ref, send_ref, router_ref,
    col_ref, whole_ref,
):
    core = where_ref[0]
    half = keep_ref.shape[1]
    own_lanes = half_lanes(core, half)
    other_lanes = half_lanes(1 - core, half)
    whole_ref[...] = dot_nn(hidden_ref[...], outer_ref[...])
    send_ref[...] = whole_ref[:, other_lanes].astype(jnp.bfloat16)
    keep_ref[...] = whole_ref[:, own_lanes]

    @pl.when(pl.program_id(0) == 0)
    def _():
        router_ref[...] = jnp.zeros_like(router_ref)
        wide = jnp.broadcast_to(row_ref[...].astype(jnp.float32), (128, row_ref.shape[1]))
        col_ref[...] = jnp.transpose(wide).astype(jnp.int32)

    router_ref[:, own_lanes] += contract_rows(logit_ref[...], own_ref[...])
    router_ref[:, other_lanes] += contract_rows(logit_ref[...], other_ref[...])


def expert_out_of(where, hidden, own, other, logit_grad, slot_row, outer):
    slots, units = hidden.shape
    tok_count = slot_row.shape[1]
    width = outer.shape[1]
    experts = logit_grad.shape[1]
    half = width // 2
    tile = 256
    halves = pl.BlockSpec((tile, half), lambda step: (step, 0))
    return pl.pallas_call(
        expert_out_kernel,
        grid=(slots // tile,),
        out_shape=[
            jax.ShapeDtypeStruct((slots, half), jnp.float32),
            jax.ShapeDtypeStruct((slots, half), jnp.bfloat16),
            hbm_out((experts, width), jnp.float32),
            hbm_out((tok_count, 128), jnp.int32),
        ],
        in_specs=[
            pl.BlockSpec(memory_space=pltpu.SMEM),
            pl.BlockSpec((tile, units), lambda step: (step, 0)),
            halves,
            halves,
            pl.BlockSpec((tile, experts), lambda step: (step, 0)),
            pl.BlockSpec((1, tok_count), lambda step: (0, 0)),
        ]
        + vmem(1),
        out_specs=[
            halves,
            halves,
            pl.BlockSpec((experts, width), lambda step: (0, 0)),
            pl.BlockSpec((tok_count, 128), lambda step: (0, 0)),
        ],
        scratch_shapes=[pltpu.VMEM((tile, width), jnp.float32)],
        compiler_params=params(),
        cost_estimate=pl.CostEstimate(
            flops=2 * slots * width * units, bytes_accessed=9000000, transcendentals=0
        ),
        name="expert_out",
    )(
        where, in_hbm(hidden), in_hbm(own), in_hbm(other), in_hbm(logit_grad), in_hbm(slot_row), outer
    )


def expert_grads_kernel(
    where_ref,
    own_hbm,
    other_hbm,
    grad_own_hbm,
    grad_other_hbm,
    hidden_ref,
    pre_grad_ref,
    router_ref,
    inner_grad_ref,
    outer_grad_ref,
    arrived_ref,
    gated_ref,
    sems,
):
    core = where_ref[0]
    half = own_hbm.shape[1]
    own_lanes = half_lanes(core, half)
    other_lanes = half_lanes(1 - core, half)

    @pl.when(pl.program_id(0) == 0)
    def _():
        copies = [
            pltpu.make_async_copy(own_hbm, arrived_ref.at[:, own_lanes], sems.at[0]),
            pltpu.make_async_copy(other_hbm, arrived_ref.at[:, other_lanes], sems.at[1]),
            pltpu.make_async_copy(grad_own_hbm, gated_ref.at[:, own_lanes], sems.at[2]),
            pltpu.make_async_copy(grad_other_hbm, gated_ref.at[:, other_lanes], sems.at[3]),
        ]
        for copy in copies:
            copy.start()
        for copy in copies:
            copy.wait()
        gate = gate_of(arrived_ref[...], router_ref[...], where_ref[1])[2]
        gated_ref[...] = (gate * gated_ref[...].astype(jnp.float32)).astype(jnp.bfloat16)

    outer_grad_ref[...] = contract_rows(hidden_ref[...], gated_ref[...])
    inner_grad_ref[...] = contract_rows(arrived_ref[...], pre_grad_ref[...])


def expert_grads(where, own, other, grad_own, grad_other, hidden, pre_grad, router):
    slots, half = own.shape
    units = hidden.shape[1]
    width = router.shape[0]
    tile = 256
    hbm = pl.BlockSpec(memory_space=pltpu.HBM)
    whole = lambda shape: pl.BlockSpec(shape, lambda step: (0, 0))
    cols = pl.BlockSpec((slots, tile), lambda step: (0, step))
    return pl.pallas_call(
        expert_grads_kernel,
        grid=(units // tile,),
        out_shape=[
            hbm_out((width, units), jnp.float32),
            hbm_out((units, width), jnp.float32),
        ],
        in_specs=[
            pl.BlockSpec(memory_space=pltpu.SMEM),
            hbm,
            hbm,
            hbm,
            hbm,
            cols,
            cols,
            whole(router.shape),
        ],
        out_specs=[
            pl.BlockSpec((width, tile), lambda step: (0, step)),
            pl.BlockSpec((tile, width), lambda step: (step, 0)),
        ],
        scratch_shapes=[
            pltpu.VMEM((slots, width), jnp.bfloat16),
            pltpu.VMEM((slots, width), jnp.bfloat16),
            pltpu.SemaphoreType.DMA((4,)),
        ],
        compiler_params=params(24),
        cost_estimate=pl.CostEstimate(
            flops=4 * slots * width * units, bytes_accessed=22000000, transcendentals=0
        ),
        name="expert_grads",
    )(
        where,
        in_hbm(own),
        in_hbm(other),
        in_hbm(grad_own),
        in_hbm(grad_other),
        in_hbm(hidden),
        in_hbm(pre_grad),
        router,
    )


def output_kernel(
    capacity, where_ref, col_ref, returned_ref, residual_ref, gain_ref, router_ref, out_ref
):
    slots, half = returned_ref.shape
    tile = residual_ref.shape[0]
    experts = router_ref.shape[1]
    col = col_ref[:, :1]
    place = lax.broadcasted_iota(jnp.int32, (tile, slots), 1)
    hot = jnp.where(place == col, 1.0, 0.0).astype(jnp.bfloat16)
    token_out = dot_nn(hot, returned_ref[...])
    residual = residual_ref[...]
    second = (residual * inverse_rms(residual) * gain_ref[...]).astype(jnp.bfloat16)
    logits = dot_nn(second, router_ref[...])
    exp_logit = jnp.exp(logits - jnp.max(logits, axis=1, keepdims=True))
    first = lax.broadcasted_iota(jnp.int32, (1, experts), 1) * capacity
    hit = jnp.where((col >= first) & (col < first + capacity), exp_logit, 0.0)
    gate = jnp.sum(hit, axis=1, keepdims=True) / jnp.sum(exp_logit, axis=1, keepdims=True)
    own = residual_ref[:, half_lanes(where_ref[0], half)]
    out_ref[...] = (own + gate * token_out).astype(jnp.bfloat16)


def output_of(where, slot_col, returned, residual, gain, router, capacity):
    tok_count, width = residual.shape
    slots, half = returned.shape
    tile = 256
    whole = lambda shape: pl.BlockSpec(shape, lambda step: (0, 0))
    return pl.pallas_call(
        partial(output_kernel, capacity),
        grid=(tok_count // tile,),
        out_shape=jax.ShapeDtypeStruct((tok_count, half), jnp.bfloat16),
        in_specs=[
            pl.BlockSpec(memory_space=pltpu.SMEM),
            pl.BlockSpec((tile, 128), lambda step: (step, 0)),
            whole(returned.shape),
            pl.BlockSpec((tile, width), lambda step: (step, 0)),
            whole((1, width)),
            whole(router.shape),
        ],
        out_specs=pl.BlockSpec((tile, half), lambda step: (step, 0)),
        compiler_params=params(),
        cost_estimate=pl.CostEstimate(
            flops=2 * tok_count * half * slots, bytes_accessed=6000000, transcendentals=0
        ),
        name="output",
    )(
        where, in_hbm(slot_col), in_hbm(returned), in_hbm(residual), gain.astype(jnp.float32)[None], router
    )


def normed_back_kernel(grads_ref, wq_ref, wk_ref, wv_ref, out_ref):
    own = wq_ref.shape[1]
    out_ref[...] = (
        dot_nt(grads_ref[:, :own], wq_ref[...])
        + dot_nt(grads_ref[:, own : 2 * own], wk_ref[...])
        + dot_nt(grads_ref[:, 2 * own :], wv_ref[...])
    ).astype(jnp.bfloat16)


def normed_back(grads, w_query, w_key, w_value):
    tok_count = grads.shape[0]
    width, own = w_query.shape
    tile = 256
    whole = pl.BlockSpec((width, own), lambda step: (0, 0))
    return pl.pallas_call(
        normed_back_kernel,
        grid=(tok_count // tile,),
        out_shape=jax.ShapeDtypeStruct((tok_count, width), jnp.bfloat16),
        in_specs=[pl.BlockSpec((tile, 3 * own), lambda step: (step, 0))] + [whole] * 3,
        out_specs=pl.BlockSpec((tile, width), lambda step: (step, 0)),
        compiler_params=params(),
        cost_estimate=pl.CostEstimate(
            flops=6 * tok_count * own * width, bytes_accessed=6000000, transcendentals=0
        ),
        name="normed_back",
    )(*(in_hbm(array) for array in (grads, w_query, w_key, w_value)))


def input_back_kernel(tokens_ref, own_ref, other_ref, gain_ref, residual_ref, out_ref):
    ybar = own_ref[...].astype(jnp.float32) + other_ref[...].astype(jnp.float32)
    values = tokens_ref[...].astype(jnp.float32)
    scale = inverse_rms(values)
    scaled = values * scale
    pulled = ybar * gain_ref[...]
    out_ref[...] = residual_ref[...] + scale * (
        pulled - scaled * jnp.mean(pulled * scaled, axis=1, keepdims=True)
    )


def input_back(tokens, own, other, gain, residual_grad):
    tok_count, width = tokens.shape
    tile = 256
    rows = pl.BlockSpec((tile, width), lambda step: (step, 0))
    return pl.pallas_call(
        input_back_kernel,
        grid=(tok_count // tile,),
        out_shape=jax.ShapeDtypeStruct((tok_count, width), jnp.float32),
        in_specs=[rows, rows, rows, pl.BlockSpec((1, width), lambda step: (0, 0)), rows],
        out_specs=rows,
        compiler_params=params(),
        cost_estimate=pl.CostEstimate(
            flops=10 * tok_count * width, bytes_accessed=11000000, transcendentals=0
        ),
        name="input_back",
    )(in_hbm(tokens), own, other, gain.astype(jnp.float32)[None], in_hbm(residual_grad))


def back_kernel(
    bits_ref,
    where_ref,
    col_hbm,
    own_hbm,
    other_hbm,
    residual_hbm,
    grad_hbm,
    wo_hbm,
    q_hbm,
    k_hbm,
    v_hbm,
    mixed_hbm,
    long_hbm,
    short_hbm,
    normed_hbm,
    wq_hbm,
    wk_hbm,
    wv_hbm,
    gain_one_ref,
    gain_two_ref,
    router_ref,
    out_hbm,
    grads_hbm,
    sent_a,
    sent_b,
    sent_c,
    kept_a,
    kept_b,
    kept_c,
    col_ref,
    back_ref,
    residual_ref,
    grad_ref,
    wo_ref,
    q_ref,
    k_ref,
    v_ref,
    mixed_ref,
    long_ref,
    short_ref,
    normed_ref,
    wq_ref,
    wk_ref,
    wv_ref,
    attn_ref,
    heads_ref,
    grads_ref,
    sg_ref,
    tiles_ref,
    far_ref,
    stack_ref,
    small_ref,
    packed_ref,
    total_ref,
    in_sems,
    out_sems,
):
    tok_count, width = residual_ref.shape
    slots, half = own_hbm.shape
    own = mixed_ref.shape[1]
    experts = router_ref.shape[0]
    pairs = own // 128
    tile = 512
    steps = tok_count // tile
    core = where_ref[0]
    first = [
        (own_hbm, back_ref.at[:, half_lanes(core, half)]),
        (other_hbm, back_ref.at[:, half_lanes(1 - core, half)]),
        (col_hbm, col_ref),
        (wo_hbm, wo_ref),
    ]
    tiles = []
    for start in range(0, tok_count, tile):
        rows = slice(start, start + tile)
        tiles.append((residual_hbm.at[rows], residual_ref.at[rows]))
        tiles.append((grad_hbm.at[rows], grad_ref.at[rows]))
    attention = [(q_hbm, q_ref), (k_hbm, k_ref), (v_hbm, v_ref), (mixed_hbm, mixed_ref), (short_hbm, short_ref)]
    for pair in range(pairs):
        both = slice(pair * 2, pair * 2 + 2)
        attention.append((long_hbm.at[both], long_ref.at[both]))
    weights = [(normed_hbm, normed_ref), (wq_hbm, wq_ref), (wk_hbm, wk_ref), (wv_hbm, wv_ref)]
    copies = start_copies(
        [
            (source, target, in_sems.at[index])
            for index, (source, target) in enumerate(first + tiles + attention + weights)
        ]
    )
    base = len(first) + len(tiles)
    outs = []

    for copy in copies[: len(first)]:
        copy.wait()
    gain_two = gain_two_ref[...]
    place = lax.broadcasted_iota(jnp.int32, (tile, slots), 1)

    def tile_out(step):
        rows = pl.ds(pl.multiple_of(step * tile, tile), tile)
        return pltpu.make_async_copy(residual_ref.at[rows], out_hbm.at[rows], out_sems.at[step])

    def one_tile(step, gain_two_grad):
        rows = pl.ds(pl.multiple_of(step * tile, tile), tile)
        at = len(first) + 2 * step
        pltpu.make_async_copy(residual_hbm.at[rows], residual_ref.at[rows], in_sems.at[at]).wait()
        pltpu.make_async_copy(grad_hbm.at[rows], grad_ref.at[rows], in_sems.at[at + 1]).wait()
        hot = jnp.where(place == col_ref[rows, :][:, :1], 1.0, 0.0).astype(jnp.bfloat16)
        ybar = dot_nn(hot, back_ref[...])
        values = residual_ref[rows, :]
        scale = inverse_rms(values)
        scaled = values * scale
        pulled = ybar * gain_two
        back = scale * (pulled - scaled * jnp.mean(pulled * scaled, axis=1, keepdims=True))
        out = back + grad_ref[rows, :].astype(jnp.float32)
        residual_ref[rows, :] = out
        attn = out.astype(jnp.bfloat16)
        attn_ref[rows, :] = attn
        heads_ref[rows, :] = dot_nt(attn, wo_ref[...]).astype(jnp.bfloat16)
        tile_out(step).start()
        return gain_two_grad + jnp.sum(ybar * scaled, axis=0, keepdims=True)

    gain_two_grad = lax.fori_loop(0, steps, one_tile, jnp.zeros((1, width), jnp.float32))
    outs += [tile_out(step) for step in range(steps)]

    for copy in copies[base : base + 5]:
        copy.wait()

    def one_pair(pair, carry):
        both = pl.ds(pair * 2, 2)
        pltpu.make_async_copy(long_hbm.at[both], long_ref.at[both], in_sems.at[base + 5 + pair]).wait()
        attend_back_pair(
            pair, heads_ref, q_ref, k_ref, v_ref, long_ref, short_ref, grads_ref, tiles_ref, far_ref,
            sg_ref,
        )
        return carry

    lax.fori_loop(0, pairs, one_pair, 0, unroll=True)
    outs += start_copies([(grads_ref, grads_hbm, out_sems.at[steps])])

    grad = contract_rows(mixed_ref[...], attn_ref[...]).astype(jnp.bfloat16)
    for part in range(width // own):
        at = 3 * width + part * own
        stack_ref[at : at + own, :] = grad[:, part * own : part * own + own]
    small_ref[0:experts, :] = router_ref[...]
    small_ref[experts + 1 : experts + 2, :] = gain_two_grad
    for head in range(2 * pairs):
        row = experts + 2 + head
        small_ref[row : row + 1, 0:512] = diagonals(tiles_ref[head])
        small_ref[row : row + 1, 512:640] = far_ref[head, 0:1, :]
        small_ref[row : row + 1, 640:768] = far_ref[head, 1:2, :]
    for copy in copies[base + 5 + pairs :]:
        copy.wait()
    rows = stack_ref.shape[0] // 3
    span = rows // 2

    def send_part(part, sent, kept):
        mine = bits_ref[part]
        sent_rows = pl.ds(pl.multiple_of(part * rows + (1 - mine) * span, span), span)
        kept_rows = pl.ds(pl.multiple_of(part * rows + mine * span, span), span)
        return start_copies(
            [
                (stack_ref.at[sent_rows], sent.at[:span], out_sems.at[steps + 4 + 2 * part]),
                (stack_ref.at[kept_rows], kept, out_sems.at[steps + 5 + 2 * part]),
            ]
        )

    span_rows = 384

    def head_rows(block, carry):
        start = pl.multiple_of(block * span_rows, span_rows)
        piece = pl.ds(start, span_rows)
        grad = contract_rows(normed_ref[:, piece], grads_ref[...])
        total = jnp.zeros((span_rows, 1), jnp.float32)
        for index, w_ref in enumerate((wq_ref, wk_ref, wv_ref)):
            part = grad[:, index * own : index * own + own]
            total = total + jnp.sum(part * w_ref[piece, :].astype(jnp.float32), axis=1, keepdims=True)
            stack_ref[pl.ds(pl.multiple_of(index * width + start, span_rows), span_rows), :] = part.astype(jnp.bfloat16)
        total_ref[piece, :] = jnp.broadcast_to(total, (span_rows, 128))
        return carry

    lax.fori_loop(0, width // span_rows, head_rows, 0)
    for part, (sent, kept) in enumerate(((sent_a, kept_a), (sent_b, kept_b))):
        outs += send_part(part, sent, kept)
    outs += send_part(2, sent_c, kept_c)
    wide = jnp.transpose(total_ref[...])
    small_ref[experts : experts + 1, :] = wide[:1, :] / gain_one_ref[...]
    small = small_ref[...]
    packed_ref[...] = jnp.concatenate([small[:, :own], small[:, own:]], axis=0).astype(jnp.bfloat16)
    outs += start_copies([(packed_ref, sent_a.at[span:], out_sems.at[steps + 3])])
    for copy in outs:
        copy.wait()


def back_pass(
    bits, where, slot_col, back_own, back_other, residual, out_grad, w_out, query_rows, key_rows,
    value_rows, mixed, long_probs, short_probs, normed, w_query, w_key, w_value, gain_one, gain_two,
    router_part,
):
    tok_count, width = normed.shape
    own = mixed.shape[1]
    slots, half = back_own.shape
    heads = long_probs.shape[0]
    count = router_part.shape[0] + 2 + heads
    span = 4 * width // 6
    tile = 512
    steps = tok_count // tile
    half_rows = hbm_out((span, own), jnp.bfloat16)
    pinned = (residual, out_grad, w_out, query_rows, key_rows, value_rows, mixed, long_probs, short_probs, normed,
              w_query, w_key, w_value)
    hbm = pl.BlockSpec(memory_space=pltpu.HBM)
    smem = pl.BlockSpec(memory_space=pltpu.SMEM)

    def scratch(array):
        return pltpu.VMEM(array.shape, array.dtype)

    flops = 2 * tok_count * width * (slots + 5 * own) + 10 * heads * (512 * 512 + 512 * 128) * 64
    out = pl.pallas_call(
        back_kernel,
        out_shape=[
            hbm_out((tok_count, width), jnp.float32),
            hbm_out((tok_count, 3 * own), jnp.bfloat16),
            hbm_out((span + 2 * count, own), jnp.bfloat16),
        ]
        + [half_rows] * 5,
        in_specs=[smem, smem] + [hbm, hbm, pl.BlockSpec(memory_space=pl.ANY)] + [hbm] * 13 + vmem(3),
        out_specs=[hbm] * 8,
        scratch_shapes=[scratch(slot_col), pltpu.VMEM((slots, width), jnp.bfloat16)]
        + [scratch(array) for array in pinned]
        + [
            pltpu.VMEM((tok_count, width), jnp.bfloat16),
            pltpu.VMEM((tok_count, own), jnp.bfloat16),
            pltpu.VMEM((tok_count, 3 * own), jnp.bfloat16),
            pltpu.VMEM((LONG_LEN, LONG_LEN), jnp.bfloat16),
            pltpu.VMEM((heads, 128, 384), jnp.float32),
            pltpu.VMEM((heads, 2, 128), jnp.float32),
            pltpu.VMEM((4 * width, own), jnp.bfloat16),
            pltpu.VMEM((count, width), jnp.float32),
            pltpu.VMEM((2 * count, own), jnp.bfloat16),
            pltpu.VMEM((width, 128), jnp.float32),
            pltpu.SemaphoreType.DMA((2 * steps + 4 + 5 + heads // 2 + 4,)),
            pltpu.SemaphoreType.DMA((steps + 10,)),
        ],
        compiler_params=params(40),
        cost_estimate=pl.CostEstimate(flops=flops, bytes_accessed=25000000, transcendentals=0),
        name="back",
    )(
        bits,
        where,
        in_hbm(slot_col),
        in_hbm(back_own),
        back_other,
        *(in_hbm(array) for array in pinned),
        gain_one.astype(jnp.float32)[None],
        gain_two.astype(jnp.float32)[None],
        router_part,
    )
    return out[0], out[1], out[2:5], out[5:]


def added(left, right):
    return (left.astype(jnp.float32) + right.astype(jnp.float32)).astype(jnp.bfloat16)


def fold_kernel(bits_ref, *refs):
    kept, got, sent, keep = refs[0:3], refs[3:6], refs[7:10], refs[10:13]
    before = refs[6]
    for part in range(3):
        span = kept[part].shape[0] // 2
        mine = bits_ref[part]
        for ref, start in ((sent[part], (1 - mine) * span), (keep[part], mine * span)):
            rows = pl.ds(pl.multiple_of(start, span), span)
            ref[:span, :] = added(kept[part][rows, :], got[part][rows, :])
    rows = kept[0].shape[0]
    sent[0][rows // 2 :, :] = added(before[rows:, :], got[0][rows:, :])


def fold(bits, kept, got, before):
    rows, lanes = kept[0].shape
    extra = before.shape[0] - rows
    half = jax.ShapeDtypeStruct((rows // 2, lanes), jnp.bfloat16)
    out = pl.pallas_call(
        fold_kernel,
        out_shape=[jax.ShapeDtypeStruct((rows // 2 + extra, lanes), jnp.bfloat16)] + [half] * 5,
        in_specs=[pl.BlockSpec(memory_space=pltpu.SMEM)] + vmem(7),
        out_specs=vmem(6),
        compiler_params=params(16),
        name="fold",
    )(bits, *kept, *got, before)
    return out[:3], out[3:]


def pack_kernel(*refs):
    kept, got, before, out = refs[0:3], refs[3:6], refs[6], refs[7]
    rows = kept[0].shape[0]
    for part in range(3):
        out[part * rows : (part + 1) * rows, :] = added(kept[part][...], got[part][:rows, :])
    out[3 * rows :, :] = added(before[rows:, :], got[0][rows:, :])


def pack(kept, got, before):
    rows, lanes = kept[0].shape
    return pl.pallas_call(
        pack_kernel,
        out_shape=jax.ShapeDtypeStruct((2 * rows + before.shape[0], lanes), jnp.bfloat16),
        in_specs=vmem(7),
        out_specs=vmem(1)[0],
        compiler_params=params(16),
        name="pack",
    )(*kept, *got, before)


def unpack_kernel(own_ref, got_ref, *out):
    rows = out[0].shape[0]
    for part in range(3):
        piece = slice(part * rows, (part + 1) * rows)
        out[part][...] = added(own_ref[piece, :], got_ref[piece, :])
    out[3][...] = own_ref[3 * rows :, :].astype(jnp.float32) + got_ref[3 * rows :, :].astype(jnp.float32)


def unpack(own, got, rows):
    lanes = own.shape[1]
    out = pl.pallas_call(
        unpack_kernel,
        out_shape=[jax.ShapeDtypeStruct((rows, lanes), jnp.bfloat16)] * 3
        + [jax.ShapeDtypeStruct((own.shape[0] - 3 * rows, lanes), jnp.float32)],
        in_specs=vmem(2),
        out_specs=vmem(4),
        compiler_params=params(16),
        name="unpack",
    )(own, got)
    return out[:3], out[3]


def join_kernel(bits_ref, *refs):
    own, got, out = refs[0:3], refs[3:6], refs[6:9]
    for part in range(3):
        span = own[part].shape[0]
        mine = bits_ref[part]
        out[part][pl.ds(pl.multiple_of(mine * span, span), span), :] = own[part][...]
        out[part][pl.ds(pl.multiple_of((1 - mine) * span, span), span), :] = got[part][...]


def join(bits, own, got):
    return pl.pallas_call(
        join_kernel,
        out_shape=[jax.ShapeDtypeStruct((p.shape[0] * 2, p.shape[1]), p.dtype) for p in own],
        in_specs=[pl.BlockSpec(memory_space=pltpu.SMEM)] + vmem(6),
        out_specs=vmem(3),
        compiler_params=params(16),
        name="join",
    )(bits, *own, *got)


def finish_kernel(bits_ref, *refs):
    own, got = refs[0:3], refs[3:6]
    results = refs[6:10]
    held, sems = refs[10:14], refs[14]
    span = own[0].shape[0]
    rows = 2 * span
    width, lanes = held[0].shape
    copies = []
    for part in range(3):
        mine = bits_ref[part]
        first = jnp.where(mine == 0, own[part][...], got[part][...])
        second = jnp.where(mine == 0, got[part][...], own[part][...])
        for base, piece in ((part * rows, first), (part * rows + span, second)):
            for index in range(3 + width // lanes):
                start = index * width if index < 3 else 3 * width + (index - 3) * lanes
                size = width if index < 3 else lanes
                low = max(start, base)
                high = min(start + size, base + span)
                if low < high:
                    values = piece[low - base : high - base, :].astype(jnp.float32)
                    if index < 3:
                        held[index][low - start : high - start, :] = values
                    else:
                        place = (index - 3) * lanes
                        held[3][low - start : high - start, place : place + lanes] = values
        for index in range(4):
            last = (index + 1) * width - 1
            if part * rows <= last < (part + 1) * rows:
                copies += start_copies([(held[index], results[index], sems.at[index])])
    for copy in copies:
        copy.wait()


def finish(bits, own, got, width):
    lanes = own[0].shape[1]
    shapes = [(width, lanes)] * 3 + [(lanes, width)]
    return pl.pallas_call(
        finish_kernel,
        out_shape=[hbm_out(shape, jnp.float32) for shape in shapes],
        in_specs=[pl.BlockSpec(memory_space=pltpu.SMEM)] + vmem(6),
        out_specs=[pl.BlockSpec(memory_space=pltpu.HBM)] * 4,
        scratch_shapes=[pltpu.VMEM(shape, jnp.float32) for shape in shapes]
        + [pltpu.SemaphoreType.DMA((4,))],
        compiler_params=params(24),
        name="finish",
    )(bits, *own, *got)


def swap_heads(rows):
    return lax.ppermute(rows, "heads", [(0, 1), (1, 0)])


def trade(rows, bit):
    count = lax.axis_size("seq")
    return lax.ppermute(rows, "seq", [(i, i ^ (1 << bit)) for i in range(count)])


def together(*groups):
    return lax.optimization_barrier(groups)


def contract_rows(left, right):
    return lax.dot_general(
        left, right, (((0,), (0,)), ((), ())), preferred_element_type=jnp.float32
    )


def on_device(
    tokens,
    gain_attn,
    w_query,
    w_key,
    w_value,
    w_out,
    bias_table,
    gain_ffn,
    w_router,
    w_inner,
    w_outer,
    routes,
    seq_lengths,
    out_grad,
):
    tok_count, width = tokens.shape
    bucket_count = bias_table.shape[0]
    experts = w_router.shape[1]
    capacity = max(2, 5 * tok_count // (4 * experts))
    senders = lax.axis_size("seq")
    bits = list(range(senders.bit_length() - 1))
    slots = experts * capacity
    half = width // 2
    own = w_query.shape[1]
    where = jnp.stack([lax.axis_index("heads"), lax.axis_index("seq")]).astype(jnp.int32)

    def exchange(rows):
        return lax.all_to_all(
            rows.reshape(senders, capacity, half), "seq", split_axis=0, concat_axis=0, tiled=True
        ).reshape(slots, half)

    def summed(keep, send):
        return (keep + swap_heads(send).astype(jnp.float32)).astype(jnp.bfloat16)

    slot_row, grad_sent = route(where, routes, out_grad, experts, capacity)
    grad_sent, tokens = together(grad_sent, tokens)
    grad_own = exchange(grad_sent)
    attn_part, normed, query_rows, key_rows, value_rows, mixed, long_probs, short_probs = attend(
        seq_lengths, tokens, gain_attn, w_query, w_key, w_value, w_out, bias_table
    )
    residual, second_sent = second_rows(
        where, tokens, attn_part, swap_heads(attn_part), gain_ffn, slot_row, slots
    )
    second_sent, grad_own = together(second_sent, grad_own)
    arrived_own = exchange(second_sent)

    inner = w_inner[0]
    outer = w_outer[0]
    grad_other = swap_heads(grad_own)
    hidden_grad = hidden_grad_of(where, grad_own, grad_other, outer)
    arrived_own, hidden_grad = together(arrived_own, hidden_grad)
    arrived_other = swap_heads(arrived_own)
    hidden, pre_grad, keep, send, logit_grad = expert(
        where, arrived_own, arrived_other, hidden_grad, inner, w_router
    )
    back_sum, hidden = together(summed(keep, send), hidden)
    back_own = exchange(back_sum)
    out_keep, out_send, router_part, slot_col = expert_out_of(
        where, hidden, arrived_own, arrived_other, logit_grad, slot_row, outer
    )
    out_sum = summed(out_keep, out_send)
    router_half = lax.dynamic_slice_in_dim(
        router_part + swap_heads(router_part), where[0] * (experts // 2), experts // 2, 0
    )
    back_own, out_sum, router_half = together(back_own, out_sum, router_half)
    back_other = swap_heads(back_own)
    returned = exchange(out_sum)

    depth = len(bits) - 1
    turns = [bits[k * depth // 3 : depth] + bits[: k * depth // 3] for k in range(3)]
    place = lax.axis_index("seq")
    mine = [jnp.stack([(place >> turn[k]) & 1 for turn in turns]).astype(jnp.int32) for k in range(depth)]
    residual_grad, head_grads, sent, kept = back_pass(
        mine[0], where, slot_col, back_own, back_other, residual, out_grad, w_out, query_rows, key_rows,
        value_rows, mixed, long_probs, short_probs, normed, w_query, w_key, w_value, gain_attn, gain_ffn,
        router_half,
    )

    def trades(arrays, k):
        return [trade(array, turn[k]) for array, turn in zip(arrays, turns)]

    for k in range(depth):
        got = trades(sent, k)
        if k == 0:
            output = output_of(where, slot_col, returned, residual, gain_ffn, w_router, capacity)
            got, output, head_grads = together(got, output, head_grads)
        if k == 1:
            normed_part = normed_back(head_grads, w_query, w_key, w_value)
            got, normed_part = together(got, normed_part)
        if k + 1 < depth:
            sent, kept = fold(mine[k + 1], kept, got, sent[0])
    normed_other = swap_heads(normed_part)
    packed = pack(kept, got, sent[0])
    packed, normed_other, pre_grad = together(packed, normed_other, pre_grad)
    got = trade(packed, bits[-1])
    inner_grad, outer_grad = expert_grads(
        where, arrived_own, arrived_other, grad_own, grad_other, hidden, pre_grad, w_router
    )
    got, inner_grad = together(got, inner_grad)
    summed_parts, small = unpack(packed, got, kept[0].shape[0])
    small = jnp.concatenate([small[: small.shape[0] // 2], small[small.shape[0] // 2 :]], axis=1)
    small_other = swap_heads(small)
    for k in reversed(range(1, depth)):
        got = trades(summed_parts, k)
        if k == depth - 1:
            got, small = together(got, small)
        if k == 1:
            lower = where[0] == 0
            own_rows, other_rows = small[: experts // 2], small_other[: experts // 2]
            router_grad = jnp.concatenate(
                [jnp.where(lower, own_rows, other_rows), jnp.where(lower, other_rows, own_rows)], axis=0
            ).T
            gain_one_grad = small[experts // 2] + small_other[experts // 2]
            gain_two_grad = small[experts // 2 + 1]
            table_grad = table_from(small[experts // 2 + 2 :], bucket_count)
            got, gain_one_grad, gain_two_grad, router_grad, table_grad = together(
                got, gain_one_grad, gain_two_grad, router_grad, table_grad
            )
        summed_parts = join(mine[k], summed_parts, got)
    got = trades(summed_parts, 0)
    input_grad = input_back(tokens, normed_part, normed_other, gain_attn, residual_grad)
    got, input_grad = together(got, input_grad)
    query_w_grad, key_w_grad, value_w_grad, out_w_grad = finish(mine[0], summed_parts, got, width)
    return (
        output,
        input_grad,
        gain_one_grad,
        query_w_grad,
        key_w_grad,
        value_w_grad,
        out_w_grad,
        table_grad,
        gain_two_grad,
        router_grad,
        inner_grad[None],
        outer_grad[None],
    )


def solution(mesh):
    in_specs = (
        P("seq", None),
        P(),
        P(None, "heads"),
        P(None, "heads"),
        P(None, "heads"),
        P("heads", None),
        P(None, "heads"),
        P(),
        P(),
        P("seq", None, "heads"),
        P("seq", "heads", None),
        P("seq", None),
        P("seq"),
        P("seq", None),
    )
    out_specs = (
        P("seq", "heads"),
        P("seq", None),
        P(),
        P(None, "heads"),
        P(None, "heads"),
        P(None, "heads"),
        P("heads", None),
        P(None, "heads"),
        P(),
        P(),
        P("seq", None, "heads"),
        P("seq", "heads", None),
    )
    return jax.shard_map(
        on_device, mesh=mesh, in_specs=in_specs, out_specs=out_specs, check_vma=False
    )
```

profile of v0, /device:TPU:0, one launch (start us, length us, event | category | flops | bytes accessed | tf_op | source)
XLA Modules:
  0.0 219.1 jit_solution(8574111926437370747)
XLA Ops:
  0.7 4.3 %route.1 = (s32[1,1024]{1,0:T(1,128)}, bf16[1280,384]{1,0:T(8,128)(2,1)}) custom-call(s32[2]{0:T(128)S(1)} %pad_add_fusion.1.where_ref, s32[1,1024]{1,0:T(1,128)} %bitcast.34, bf16[1024,768]{1,0:T(8,128)(2,1)} %grad_hbm.3), custom_call_target="tpu_custom_call" | custom-call | flops 1006632960 | bytes 4000000 | tf_op jit(solution)/shard_map/route/pallas_call | solution.py:475
  5.0 8.3 %all-to-all-start = ((bf16[16,80,384]{2,1,0:T(8,128)(2,1)}), bf16[16,80,384]{2,1,0:T(8,128)(2,1)S(1)}, u32[]{:S(2)}, u32[]{:S(2)}) async-start(bf16[16,80,384]{2,1,0:T(8,128)(2,1)} %bitcast.7), calls=%async_computation | async-start | bytes 1966080 | tf_op jit(solution)/shard_map/all_to_all | solution.py:1395
  13.4 11.8 %attend.1 = (bf16[1024,768]{1,0:T(8,128)(2,1)S(1)}, bf16[1024,768]{1,0:T(8,128)(2,1)}, bf16[1024,384]{1,0:T(8,128)(2,1)}, bf16[1024,384]{1,0:T(8,128)(2,1)}, bf1...) custom-call(s32[5]{0:T(128)S(1)} %copy-done.10, ...), custom_call_target="tpu_custom_call" | custom-call | flops 2919235584 | bytes 16000000 | tf_op jit(solution)/shard_map/attend/pallas_call | solution.py:289
  25.4 3.4 %collective-permute-done.other_ref = bf16[1024,768]{1,0:T(8,128)(2,1)S(1)} collective-permute-done((bf16[1024,768]{1,0:T(8,128)(2,1)S(1)}, bf16[1024,768]{1,0:T(8,128)(2,1)S(1)}, u32[]{:S(2)}, u32[]{:S(2)}) %collective-permute-start) | collective-permute-done | bytes 1572896 | tf_op jit(solution)/shard_map/ppermute | solution.py:1349
  28.7 5.4 %second.1 = (f32[1024,768]{1,0:T(8,128)}, bf16[1280,384]{1,0:T(8,128)(2,1)}) custom-call(s32[2]{0:T(128)S(1)} %pad_add_fusion.1.where_ref, bf16[1024,768]{1,0:T(8,128)(2,1)} %tokens_ref, bf16[1024,768]{1,0:T(8,128)(2,1)S(1)} %get-tuple-element.111.own_ref, bf16[1024,768]{1,0:T(8,128)(2,1)S(1)} %collective-permute-done.other_ref, ...), custom_call_target="tpu_custom_call" | custom-call | flops 1006632960 | bytes 13000000 | tf_op jit(solution)/shard_map/second/pallas_call | solution.py:536
  34.1 2.4 %all-to-all-done = bf16[16,80,384]{2,1,0:T(8,128)(2,1)S(1)} async-done(((bf16[16,80,384]{2,1,0:T(8,128)(2,1)}), bf16[16,80,384]{2,1,0:T(8,128)(2,1)S(1)}, u32[]{:S(2)}, u32[]{:S(2)}) %all-to-all-start) | async-done | bytes 983072 | tf_op jit(solution)/shard_map/all_to_all | solution.py:1395
  36.6 5.7 %all-to-all-start.1 = ((bf16[16,80,384]{2,1,0:T(8,128)(2,1)}), bf16[16,80,384]{2,1,0:T(8,128)(2,1)S(1)}, u32[]{:S(2)}, u32[]{:S(2)}) async-start(bf16[16,80,384]{2,1,0:T(8,128)(2,1)} %bitcast.9), calls=%async_computation.1 | async-start | bytes 1966080 | tf_op jit(solution)/shard_map/all_to_all | solution.py:1395
  42.3 2.6 %collective-permute-done.1.other_ref.grad_other_hbm = bf16[1280,384]{1,0:T(8,128)(2,1)S(1)} collective-permute-done((bf16[1280,384]{1,0:T(8,128)(2,1)S(1)}, bf16[1280,384]{1,0:T(8,128)(2,1)S(1)}, u32[]{:S(2)}, u32[]{:S(2)}) %collective-permute-start.1) | collective-permute-done | bytes 983072 | tf_op jit(solution)/shard_map/ppermute | solution.py:1349
  44.9 2.0 copy-done.6
  46.9 5.6 %hidden_grad.1.hg_ref = bf16[1280,1536]{1,0:T(8,128)(2,1)} custom-call(s32[2]{0:T(128)S(1)} %pad_add_fusion.1.where_ref, bf16[1280,384]{1,0:T(8,128)(2,1)S(1)} %bitcast.22, bf16[1280,384]{1,0:T(8,128)(2,1)S(1)} %collective-permute-done.1.other_ref.grad_other_hbm, bf16[1536,768]{1,0:T(8,128)(2,1)S(1)} %bitcast.28), custom_call_target="tpu_custom_call" | custom-call | flops 3019898880 | bytes 12000000 | tf_op jit(solution)/shard_map/hidden_grad/pallas_call | solution.py:573
  52.6 12.0 %all-to-all-done.1 = bf16[16,80,384]{2,1,0:T(8,128)(2,1)S(1)} async-done(((bf16[16,80,384]{2,1,0:T(8,128)(2,1)}), bf16[16,80,384]{2,1,0:T(8,128)(2,1)S(1)}, u32[]{:S(2)}, u32[]{:S(2)}) %all-to-all-start.1) | async-done | bytes 983072 | tf_op jit(solution)/shard_map/all_to_all | solution.py:1395
  64.7 2.4 %collective-permute-done.2.other_ref.other_hbm = bf16[1280,384]{1,0:T(8,128)(2,1)S(1)} collective-permute-done((bf16[1280,384]{1,0:T(8,128)(2,1)S(1)}, bf16[1280,384]{1,0:T(8,128)(2,1)S(1)}, u32[]{:S(2)}, u32[]{:S(2)}) %collective-permute-start.2) | collective-permute-done | bytes 983072 | tf_op jit(solution)/shard_map/ppermute | solution.py:1349
  67.1 14.7 %expert.1 = (bf16[1280,1536]{1,0:T(8,128)(2,1)}, bf16[1280,1536]{1,0:T(8,128)(2,1)}, f32[1280,384]{1,0:T(8,128)S(1)}, bf16[1280,384]{1,0:T(8,128)(2,1)S(1)}, bf16[1280,16]{1,0:T(8,128)(2,1)}) custom-call(s32[2]{0:T(128)S(1)} %pad_add_fusion.1.where_ref, bf16[1280,384]{1,0:T(8,128)(2,1)S(1)} %bitcast.25, ...), custom_call_target="tpu_custom_call" | custom-call | flops 6039797760 | bytes 20000000 | tf_op jit(solution)/shard_map/expert/pallas_call | solution.py:650
  82.1 2.4 %collective-permute-done.3 = bf16[1280,384]{1,0:T(8,128)(2,1)S(1)} collective-permute-done((bf16[1280,384]{1,0:T(8,128)(2,1)S(1)}, bf16[1280,384]{1,0:T(8,128)(2,1)S(1)}, u32[]{:S(2)}, u32[]{:S(2)}) %collective-permute-start.3) | collective-permute-done | bytes 983072 | tf_op jit(solution)/shard_map/ppermute | solution.py:1349
  84.5 1.2 add_convert_fusion.1
  85.7 5.7 %all-to-all-start.2 = ((bf16[16,80,384]{2,1,0:T(8,128)(2,1)}), bf16[16,80,384]{2,1,0:T(8,128)(2,1)}, u32[]{:S(2)}, u32[]{:S(2)}) async-start(bf16[16,80,384]{2,1,0:T(8,128)(2,1)} %bitcast.13), calls=%async_computation.2 | async-start | bytes 1966080 | tf_op jit(solution)/shard_map/all_to_all | solution.py:1395
  91.5 1.7 copy-done.7
  93.1 8.0 %expert_out.1 = (f32[1280,384]{1,0:T(8,128)S(1)}, bf16[1280,384]{1,0:T(8,128)(2,1)S(1)}, f32[16,768]{1,0:T(8,128)}, s32[1024,128]{1,0:T(8,128)}) custom-call(s32[2]{0:T(128)S(1)} %pad_add_fusion.1.where_ref, bf16[1280,1536]{1,0:T(8,128)(2,1)} %get-tuple-element.122.hidden_ref, bf16[1280,384]{1,0:T(8,128)(2,1)} %bitcast.26, bf16[1280,384]{1,0:T(8,128)(2,1)} %copy-done.9, ...), custom_call_target="tpu_custom_call" | custom-call | flops 3019898880 | bytes 9000000 | tf_op jit(solution)/shard_map/expert_out/pallas_call | solution.py:717
  101.6 2.0 collective-permute-done.5
  104.3 2.3 %add_convert_fusion = bf16[1280,384]{1,0:T(8,128)(2,1)} fusion(f32[1280,384]{1,0:T(8,128)S(1)} %get-tuple-element.126, bf16[1280,384]{1,0:T(8,128)(2,1)} %collective-permute-done.4), kind=kLoop, calls=%fused_computation | loop fusion | flops 1474560 | bytes 3932160 | tf_op jit(solution)/shard_map/convert_element_type | solution.py:1400
  106.7 8.3 %all-to-all-done.2 = bf16[16,80,384]{2,1,0:T(8,128)(2,1)} async-done(((bf16[16,80,384]{2,1,0:T(8,128)(2,1)}), bf16[16,80,384]{2,1,0:T(8,128)(2,1)}, u32[]{:S(2)}, u32[]{:S(2)}) %all-to-all-start.2) | async-done | bytes 983072 | tf_op jit(solution)/shard_map/all_to_all | solution.py:1395
  115.0 5.8 %all-to-all-start.3 = ((bf16[16,80,384]{2,1,0:T(8,128)(2,1)}), bf16[16,80,384]{2,1,0:T(8,128)(2,1)S(1)}, u32[]{:S(2)}, u32[]{:S(2)}) async-start(bf16[16,80,384]{2,1,0:T(8,128)(2,1)} %bitcast.31), calls=%async_computation.3 | async-start | bytes 1966080 | tf_op jit(solution)/shard_map/all_to_all | solution.py:1395
  120.8 20.7 %back.1 = (f32[1024,768]{1,0:T(8,128)}, bf16[1024,1152]{1,0:T(8,128)(2,1)}, bf16[544,384]{1,0:T(8,128)(2,1)}, bf16[512,384]{1,0:T(8,128)(2,1)}, bf16[512,384]{1,...) custom-call(s32[3]{0:T(128)S(1)} %pad_add_fusion.bits_ref, ...), custom_call_target="tpu_custom_call" | custom-call | flops 6291456000 | bytes 25000000 | tf_op jit(solution)/shard_map/back/pallas_call | solution.py:1163
  141.6 2.0 collective-permute-start.7
  143.6 1.5 collective-permute-start.8
  145.0 1.4 collective-permute-start.9
  146.6 0.9 copy-done.11
  147.5 6.2 %output.1 = bf16[1024,384]{1,0:T(8,128)(2,1)} custom-call(s32[2]{0:T(128)S(1)} %pad_add_fusion.1.where_ref, s32[1024,128]{1,0:T(8,128)} %get-tuple-element.124.col_hbm.col_ref, bf16[1280,384]{1,0:T(8,128)(2,1)} %bitcast.30, f32[1024,768]{1,0:T(8,128)} %get-tuple-element.130.residual_hbm.residual_ref, f32[1,768]{1,0:T(1,128)S(1)} %reshape.103.gain_ref.gain_two_ref, ...), custom_call_target="tpu_custom_call" | custom-call | flops 1006632960 | bytes 6000000 | tf_op jit(solution)/shard_map/output/pallas_call | solution.py:868
  154.5 1.2 collective-permute-done.9.refs_5_
  157.2 1.5 collective-permute-start.11
  159.4 5.1 %normed_back.1.own_ref = bf16[1024,768]{1,0:T(8,128)(2,1)S(1)} custom-call(bf16[1024,1152]{1,0:T(8,128)(2,1)} %get-tuple-element.157.grads_ref, bf16[768,384]{1,0:T(8,128)(2,1)} %wq_ref.1, bf16[768,384]{1,0:T(8,128)(2,1)} %wk_ref.1, bf16[768,384]{1,0:T(8,128)(2,1)} %wv_ref.1), custom_call_target="tpu_custom_call" | custom-call | flops 1811939328 | bytes 6000000 | tf_op jit(solution)/shard_map/normed_back/pallas_call | solution.py:905
  166.0 1.3 collective-permute-start.14
  167.3 1.5 collective-permute-start.15
  168.8 2.3 %collective-permute-done.14.refs_4_ = bf16[128,384]{1,0:T(8,128)(2,1)S(1)} collective-permute-done((bf16[128,384]{1,0:T(8,128)(2,1)S(1)}, bf16[128,384]{1,0:T(8,128)(2,1)S(1)}, u32[]{:S(2)}, u32[]{:S(2)}) %collective-permute-start.14) | collective-permute-done | bytes 98336 | tf_op jit(solution)/shard_map/ppermute | solution.py:1354
  172.0 2.4 %collective-permute-start.17 = (bf16[416,384]{1,0:T(8,128)(2,1)S(1)}, bf16[416,384]{1,0:T(8,128)(2,1)S(1)}, u32[]{:S(2)}, u32[]{:S(2)}) collective-permute-start(bf16[416,384]{1,0:T(8,128)(2,1)S(1)} %pack.1.own_ref), channel_id=1, source_target_pairs={{0,8},{1,9},{2,10},{3,11},{4,12},{5,13},{6,14},{7,15},{8,0},{9,1},... | collective-permute-start | bytes 958472 | tf_op jit(solution)/shard_map/ppermute | solution.py:1354
  174.5 13.7 %expert_grads.1 = (f32[768,1536]{1,0:T(8,128)}, f32[1536,768]{1,0:T(8,128)}) custom-call(s32[2]{0:T(128)S(1)} %pad_add_fusion.1.where_ref, bf16[1280,384]{1,0:T(8,128)(2,1)} %bitcast.27, bf16[1280,384]{1,0:T(8,128)(2,1)} %copy-done.9, bf16[1280,384]{1,0:T(8,128)(2,1)} %bitcast.23, bf16[1280,384]{1,0:T(8,128)(2,1)} %copy-done.8, ...), custom_call_target="tpu_custom_call" | custom-call | flops 6039797760 | bytes 22000000 | tf_op jit(solution)/shard_map/expert_grads/pallas_call | solution.py:799
  189.3 1.1 collective-permute-start.18
  190.9 1.5 collective-permute-start.20
  193.0 1.5 collective-permute-done.18.refs_3_
  195.7 1.0 join.2
  196.7 1.5 collective-permute-start.21
  198.2 1.3 collective-permute-start.22
  201.8 1.4 slice_reduce_fusion
  203.2 1.7 fusion
  207.6 1.1 collective-permute-start.27
  208.7 5.2 %input_back.1 = f32[1024,768]{1,0:T(8,128)} custom-call(bf16[1024,768]{1,0:T(8,128)(2,1)} %tokens_ref, bf16[1024,768]{1,0:T(8,128)(2,1)S(1)} %normed_back.1.own_ref, bf16[1024,768]{1,0:T(8,128)(2,1)S(1)} %collective-permute-done.16.other_ref, f32[1,768]{1,0:T(1,128)S(1)} %reshape.102.gain_ref.gain_one_ref, f32[1024,768]{1,0:T(8,128)} %get-tuple-element.191.residual_ref), custom_call_target="tpu_custom_call" | custom-call | flops 7864320 | bytes 11000000 | tf_op jit(solution)/shard_map/input_back/pallas_call | solution.py:934
  213.8 1.1 collective-permute-done.25.refs_3_
  216.1 2.8 %finish.1 = (f32[768,384]{1,0:T(8,128)}, f32[768,384]{1,0:T(8,128)}, f32[768,384]{1,0:T(8,128)}, f32[384,768]{1,0:T(8,128)}) custom-call(s32[3]{0:T(128)S(1)} %pad_add_fusion.bits_ref, bf16[512,384]{1,0:T(8,128)(2,1)S(1)} %get-tuple-element.187.refs_0_, bf16[512,384]{1,0:T(8,128)(2,1)S(1)} %get-tuple-element.188.refs_1_, ...), custom_call_target="tpu_custom_call" | custom-call | tf_op jit(solution)/shard_map/finish/pallas_call | solution.py:1336
  (84 shorter events, 17.0 us)
Async XLA Ops:
  0.7 12.7 %copy-start.13 = (bf16[768]{0:T(1024)(128)(2,1)S(1)}, bf16[768]{0:T(1024)(128)(2,1)}, u32[]{:S(2)}) copy-start(bf16[768]{0:T(1024)(128)(2,1)} %param.15) | copy-start | bytes 4612
  0.7 12.7 %copy-start.14 = (bf16[32,6]{0,1:T(8,128)(2,1)S(1)}, bf16[32,6]{0,1:T(8,128)(2,1)}, u32[]{:S(2)}) copy-start(bf16[32,6]{0,1:T(8,128)(2,1)} %param.20) | copy-start | bytes 1156
  0.7 12.7 %copy-start.10 = (s32[5]{0:T(128)S(1)}, s32[5]{0:T(128)}, u32[]{:S(2)}) copy-start(s32[5]{0:T(128)} %lengths_ref.1) | copy-start | bytes 64
  5.0 31.5 %all-to-all-start = ((bf16[16,80,384]{2,1,0:T(8,128)(2,1)}), bf16[16,80,384]{2,1,0:T(8,128)(2,1)S(1)}, u32[]{:S(2)}, u32[]{:S(2)}) async-start(bf16[16,80,384]{2,1,0:T(8,128)(2,1)} %bitcast.7), calls=%async_computation | async-start | bytes 1966080 | tf_op jit(solution)/shard_map/all_to_all | solution.py:1395
  13.4 11.9 %copy-start.15 = (bf16[768]{0:T(1024)(128)(2,1)S(1)}, bf16[768]{0:T(1024)(128)(2,1)}, u32[]{:S(2)}) copy-start(bf16[768]{0:T(1024)(128)(2,1)} %param.21) | copy-start | bytes 4612
  25.3 3.5 %collective-permute-start = (bf16[1024,768]{1,0:T(8,128)(2,1)S(1)}, bf16[1024,768]{1,0:T(8,128)(2,1)S(1)}, u32[]{:S(2)}, u32[]{:S(2)}) collective-permute-start(bf16[1024,768]{1,0:T(8,128)(2,1)S(1)} %get-tuple-element.111.own_ref), channel_id=1, source_target_pairs={{0,16},{16,0},{1,17},{17,1},{2,18},{18,2},{3,19},{19,3},{4,20},{20... | collective-permute-start | bytes 4718600 | tf_op jit(solution)/shard_map/ppermute | solution.py:1349
  36.6 16.0 %copy-start = (bf16[16,80,384]{2,1,0:T(8,128)(2,1)}, bf16[16,80,384]{2,1,0:T(8,128)(2,1)S(1)}, u32[]{:S(2)}) copy-start(bf16[16,80,384]{2,1,0:T(8,128)(2,1)S(1)} %all-to-all-done) | copy-start | bytes 2949124
  36.6 28.0 %all-to-all-start.1 = ((bf16[16,80,384]{2,1,0:T(8,128)(2,1)}), bf16[16,80,384]{2,1,0:T(8,128)(2,1)S(1)}, u32[]{:S(2)}, u32[]{:S(2)}) async-start(bf16[16,80,384]{2,1,0:T(8,128)(2,1)} %bitcast.9), calls=%async_computation.1 | async-start | bytes 1966080 | tf_op jit(solution)/shard_map/all_to_all | solution.py:1395
  42.3 2.6 %collective-permute-start.1 = (bf16[1280,384]{1,0:T(8,128)(2,1)S(1)}, bf16[1280,384]{1,0:T(8,128)(2,1)S(1)}, u32[]{:S(2)}, u32[]{:S(2)}) collective-permute-start(bf16[1280,384]{1,0:T(8,128)(2,1)S(1)} %bitcast.21), channel_id=1, source_target_pairs={{0,16},{16,0},{1,17},{17,1},{2,18},{18,2},{3,19},{19,3},{4,20},{20... | collective-permute-start | bytes 2949128 | tf_op jit(solution)/shard_map/ppermute | solution.py:1349
  44.9 7.7 %copy-start.8 = (bf16[1280,384]{1,0:T(8,128)(2,1)}, bf16[1280,384]{1,0:T(8,128)(2,1)S(1)}, u32[]{:S(2)}) copy-start(bf16[1280,384]{1,0:T(8,128)(2,1)S(1)} %collective-permute-done.1.other_ref.grad_other_hbm) | copy-start | bytes 2949124
  44.9 2.0 copy-start.6
  46.9 17.7 %copy-start.12 = (bf16[768,16]{0,1:T(8,128)(2,1)S(1)}, bf16[768,16]{0,1:T(8,128)(2,1)}, u32[]{:S(2)}) copy-start(bf16[768,16]{0,1:T(8,128)(2,1)} %param.22) | copy-start | bytes 73732
  64.6 17.3 %copy-start.1 = (bf16[16,80,384]{2,1,0:T(8,128)(2,1)}, bf16[16,80,384]{2,1,0:T(8,128)(2,1)S(1)}, u32[]{:S(2)}) copy-start(bf16[16,80,384]{2,1,0:T(8,128)(2,1)S(1)} %all-to-all-done.1) | copy-start | bytes 2949124
  64.6 2.6 %collective-permute-start.2 = (bf16[1280,384]{1,0:T(8,128)(2,1)S(1)}, bf16[1280,384]{1,0:T(8,128)(2,1)S(1)}, u32[]{:S(2)}, u32[]{:S(2)}) collective-permute-start(bf16[1280,384]{1,0:T(8,128)(2,1)S(1)} %bitcast.24), channel_id=1, source_target_pairs={{0,16},{16,0},{1,17},{17,1},{2,18},{18,2},{3,19},{19,3},{4,20},{20... | collective-permute-start | bytes 2949128 | tf_op jit(solution)/shard_map/ppermute | solution.py:1349
  67.1 14.7 %copy-start.9 = (bf16[1280,384]{1,0:T(8,128)(2,1)}, bf16[1280,384]{1,0:T(8,128)(2,1)S(1)}, u32[]{:S(2)}) copy-start(bf16[1280,384]{1,0:T(8,128)(2,1)S(1)} %collective-permute-done.2.other_ref.other_hbm) | copy-start | bytes 2949124
  81.9 2.6 %collective-permute-start.3 = (bf16[1280,384]{1,0:T(8,128)(2,1)S(1)}, bf16[1280,384]{1,0:T(8,128)(2,1)S(1)}, u32[]{:S(2)}, u32[]{:S(2)}) collective-permute-start(bf16[1280,384]{1,0:T(8,128)(2,1)S(1)} %get-tuple-element.120), channel_id=1, source_target_pairs={{0,16},{16,0},{1,17},{17,1},{2,18},{18,2},{3,19},{19,3},{4,20},{20... | collective-permute-start | bytes 2949128 | tf_op jit(solution)/shard_map/ppermute | solution.py:1349
  85.7 29.2 %all-to-all-start.2 = ((bf16[16,80,384]{2,1,0:T(8,128)(2,1)}), bf16[16,80,384]{2,1,0:T(8,128)(2,1)}, u32[]{:S(2)}, u32[]{:S(2)}) async-start(bf16[16,80,384]{2,1,0:T(8,128)(2,1)} %bitcast.13), calls=%async_computation.2 | async-start | bytes 1966080 | tf_op jit(solution)/shard_map/all_to_all | solution.py:1395
  91.5 1.7 copy-start.7
  101.1 3.2 %collective-permute-start.4 = (bf16[1280,384]{1,0:T(8,128)(2,1)S(1)}, bf16[1280,384]{1,0:T(8,128)(2,1)}, u32[]{:S(2)}, u32[]{:S(2)}) collective-permute-start(bf16[1280,384]{1,0:T(8,128)(2,1)S(1)} %get-tuple-element.127), channel_id=1, source_target_pairs={{0,16},{16,0},{1,17},{17,1},{2,18},{18,2},{3,19},{19,3},{4,20},{20... | collective-permute-start | bytes 2949128 | tf_op jit(solution)/shard_map/ppermute | solution.py:1349
  101.1 2.5 %collective-permute-start.5 = (f32[16,768]{1,0:T(8,128)}, f32[16,768]{1,0:T(8,128)S(1)}, u32[]{:S(2)}, u32[]{:S(2)}) collective-permute-start(f32[16,768]{1,0:T(8,128)} %get-tuple-element.128), channel_id=1, source_target_pairs={{0,16},{16,0},{1,17},{17,1},{2,18},{18,2},{3,19},{19,3},{4,20},{20... | collective-permute-start | bytes 147464 | tf_op jit(solution)/shard_map/ppermute | solution.py:1349
  114.9 5.9 %collective-permute-start.6 = (bf16[1280,384]{1,0:T(8,128)(2,1)}, bf16[1280,384]{1,0:T(8,128)(2,1)S(1)}, u32[]{:S(2)}, u32[]{:S(2)}) collective-permute-start(bf16[1280,384]{1,0:T(8,128)(2,1)} %bitcast.14.own_hbm), channel_id=1, source_target_pairs={{0,16},{16,0},{1,17},{17,1},{2,18},{18,2},{3,19},{19,3},{4,20},{20... | collective-permute-start | bytes 2949128 | tf_op jit(solution)/shard_map/ppermute | solution.py:1349
  115.0 31.6 %all-to-all-start.3 = ((bf16[16,80,384]{2,1,0:T(8,128)(2,1)}), bf16[16,80,384]{2,1,0:T(8,128)(2,1)S(1)}, u32[]{:S(2)}, u32[]{:S(2)}) async-start(bf16[16,80,384]{2,1,0:T(8,128)(2,1)} %bitcast.31), calls=%async_computation.3 | async-start | bytes 1966080 | tf_op jit(solution)/shard_map/all_to_all | solution.py:1395
  141.6 14.1 %collective-permute-start.7 = (bf16[544,384]{1,0:T(8,128)(2,1)}, bf16[544,384]{1,0:T(8,128)(2,1)S(1)}, u32[]{:S(2)}, u32[]{:S(2)}) collective-permute-start(bf16[544,384]{1,0:T(8,128)(2,1)} %get-tuple-element.139.refs_6_), channel_id=1, source_target_pairs={{0,1},{1,0},{2,3},{3,2},{4,5},{5,4},{6,7},{7,6},{8,9},{9,8},{10,11... | collective-permute-start | bytes 1253384 | tf_op jit(solution)/shard_map/ppermute | solution.py:1354
  143.6 10.9 %collective-permute-start.8 = (bf16[512,384]{1,0:T(8,128)(2,1)}, bf16[512,384]{1,0:T(8,128)(2,1)S(1)}, u32[]{:S(2)}, u32[]{:S(2)}) collective-permute-start(bf16[512,384]{1,0:T(8,128)(2,1)} %get-tuple-element.140), channel_id=1, source_target_pairs={{0,2},{1,3},{2,0},{3,1},{4,6},{5,7},{6,4},{7,5},{8,10},{9,11},{10,... | collective-permute-start | bytes 1179656 | tf_op jit(solution)/shard_map/ppermute | solution.py:1354
  145.0 10.6 %collective-permute-start.9 = (bf16[512,384]{1,0:T(8,128)(2,1)}, bf16[512,384]{1,0:T(8,128)(2,1)S(1)}, u32[]{:S(2)}, u32[]{:S(2)}) collective-permute-start(bf16[512,384]{1,0:T(8,128)(2,1)} %get-tuple-element.141), channel_id=1, source_target_pairs={{0,4},{1,5},{2,6},{3,7},{4,0},{5,1},{6,2},{7,3},{8,12},{9,13},{10,... | collective-permute-start | bytes 1179656 | tf_op jit(solution)/shard_map/ppermute | solution.py:1354
  146.6 0.9 copy-start.11
  147.5 8.1 %copy-start.2 = (bf16[544,384]{1,0:T(8,128)(2,1)S(1)}, bf16[544,384]{1,0:T(8,128)(2,1)}, u32[]{:S(2)}) copy-start(bf16[544,384]{1,0:T(8,128)(2,1)} %get-tuple-element.139.refs_6_) | copy-start | bytes 1253380
  147.5 8.1 %copy-start.3 = (bf16[512,384]{1,0:T(8,128)(2,1)S(1)}, bf16[512,384]{1,0:T(8,128)(2,1)}, u32[]{:S(2)}) copy-start(bf16[512,384]{1,0:T(8,128)(2,1)} %get-tuple-element.145.refs_0_) | copy-start | bytes 1179652
  147.5 8.2 %copy-start.4 = (bf16[512,384]{1,0:T(8,128)(2,1)S(1)}, bf16[512,384]{1,0:T(8,128)(2,1)}, u32[]{:S(2)}) copy-start(bf16[512,384]{1,0:T(8,128)(2,1)} %get-tuple-element.146.refs_1_) | copy-start | bytes 1179652
  147.5 8.2 %copy-start.5 = (bf16[512,384]{1,0:T(8,128)(2,1)S(1)}, bf16[512,384]{1,0:T(8,128)(2,1)}, u32[]{:S(2)}) copy-start(bf16[512,384]{1,0:T(8,128)(2,1)} %get-tuple-element.147.refs_2_) | copy-start | bytes 1179652
  156.5 8.3 %collective-permute-start.10 = (bf16[288,384]{1,0:T(8,128)(2,1)S(1)}, bf16[288,384]{1,0:T(8,128)(2,1)S(1)}, u32[]{:S(2)}, u32[]{:S(2)}) collective-permute-start(bf16[288,384]{1,0:T(8,128)(2,1)S(1)} %get-tuple-element.154.refs_6_), channel_id=1, source_target_pairs={{0,2},{1,3},{2,0},{3,1},{4,6},{5,7},{6,4},{7,5},{8,10},{9,11},{10,... | collective-permute-start | bytes 663560 | tf_op jit(solution)/shard_map/ppermute | solution.py:1354
  157.2 7.4 %collective-permute-start.11 = (bf16[256,384]{1,0:T(8,128)(2,1)S(1)}, bf16[256,384]{1,0:T(8,128)(2,1)S(1)}, u32[]{:S(2)}, u32[]{:S(2)}) collective-permute-start(bf16[256,384]{1,0:T(8,128)(2,1)S(1)} %get-tuple-element.155), channel_id=1, source_target_pairs={{0,4},{1,5},{2,6},{3,7},{4,0},{5,1},{6,2},{7,3},{8,12},{9,13},{10,... | collective-permute-start | bytes 589832 | tf_op jit(solution)/shard_map/ppermute | solution.py:1354
  158.6 6.2 %collective-permute-start.12 = (bf16[256,384]{1,0:T(8,128)(2,1)S(1)}, bf16[256,384]{1,0:T(8,128)(2,1)S(1)}, u32[]{:S(2)}, u32[]{:S(2)}) collective-permute-start(bf16[256,384]{1,0:T(8,128)(2,1)S(1)} %get-tuple-element.156), channel_id=1, source_target_pairs={{0,1},{1,0},{2,3},{3,2},{4,5},{5,4},{6,7},{7,6},{8,9},{9,8},{10,11... | collective-permute-start | bytes 589832 | tf_op jit(solution)/shard_map/ppermute | solution.py:1354
  164.9 7.1 %collective-permute-start.16 = (bf16[1024,768]{1,0:T(8,128)(2,1)S(1)}, bf16[1024,768]{1,0:T(8,128)(2,1)S(1)}, u32[]{:S(2)}, u32[]{:S(2)}) collective-permute-start(bf16[1024,768]{1,0:T(8,128)(2,1)S(1)} %normed_back.1.own_ref), channel_id=1, source_target_pairs={{0,16},{16,0},{1,17},{17,1},{2,18},{18,2},{3,19},{19,3},{4,20},{20... | collective-permute-start | bytes 4718600 | tf_op jit(solution)/shard_map/ppermute | solution.py:1349
  165.7 6.3 %collective-permute-start.13 = (bf16[160,384]{1,0:T(8,128)(2,1)S(1)}, bf16[160,384]{1,0:T(8,128)(2,1)S(1)}, u32[]{:S(2)}, u32[]{:S(2)}) collective-permute-start(bf16[160,384]{1,0:T(8,128)(2,1)S(1)} %get-tuple-element.164.refs_6_), channel_id=1, source_target_pairs={{0,4},{1,5},{2,6},{3,7},{4,0},{5,1},{6,2},{7,3},{8,12},{9,13},{10,... | collective-permute-start | bytes 368648 | tf_op jit(solution)/shard_map/ppermute | solution.py:1354
  166.0 5.0 %collective-permute-start.14 = (bf16[128,384]{1,0:T(8,128)(2,1)S(1)}, bf16[128,384]{1,0:T(8,128)(2,1)S(1)}, u32[]{:S(2)}, u32[]{:S(2)}) collective-permute-start(bf16[128,384]{1,0:T(8,128)(2,1)S(1)} %get-tuple-element.165), channel_id=1, source_target_pairs={{0,1},{1,0},{2,3},{3,2},{4,5},{5,4},{6,7},{7,6},{8,9},{9,8},{10,11... | collective-permute-start | bytes 294920 | tf_op jit(solution)/shard_map/ppermute | solution.py:1354
  167.3 4.6 %collective-permute-start.15 = (bf16[128,384]{1,0:T(8,128)(2,1)S(1)}, bf16[128,384]{1,0:T(8,128)(2,1)S(1)}, u32[]{:S(2)}, u32[]{:S(2)}) collective-permute-start(bf16[128,384]{1,0:T(8,128)(2,1)S(1)} %get-tuple-element.166), channel_id=1, source_target_pairs={{0,2},{1,3},{2,0},{3,1},{4,6},{5,7},{6,4},{7,5},{8,10},{9,11},{10,... | collective-permute-start | bytes 294920 | tf_op jit(solution)/shard_map/ppermute | solution.py:1354
  172.0 16.5 %collective-permute-start.17 = (bf16[416,384]{1,0:T(8,128)(2,1)S(1)}, bf16[416,384]{1,0:T(8,128)(2,1)S(1)}, u32[]{:S(2)}, u32[]{:S(2)}) collective-permute-start(bf16[416,384]{1,0:T(8,128)(2,1)S(1)} %pack.1.own_ref), channel_id=1, source_target_pairs={{0,8},{1,9},{2,10},{3,11},{4,12},{5,13},{6,14},{7,15},{8,0},{9,1},... | collective-permute-start | bytes 958472 | tf_op jit(solution)/shard_map/ppermute | solution.py:1354
  189.3 11.2 %collective-permute-start.24 = (f32[16,768]{1,0:T(8,128)}, f32[16,768]{1,0:T(8,128)}, u32[]{:S(2)}, u32[]{:S(2)}) collective-permute-start(f32[16,768]{1,0:T(8,128)} %pad_maximum_fusion), channel_id=1, source_target_pairs={{0,16},{16,0},{1,17},{17,1},{2,18},{18,2},{3,19},{19,3},{4,20},{20... | collective-permute-start | bytes 147464 | tf_op jit(solution)/shard_map/ppermute | solution.py:1349
  189.3 5.2 %collective-permute-start.18 = (bf16[128,384]{1,0:T(8,128)(2,1)S(1)}, bf16[128,384]{1,0:T(8,128)(2,1)S(1)}, u32[]{:S(2)}, u32[]{:S(2)}) collective-permute-start(bf16[128,384]{1,0:T(8,128)(2,1)S(1)} %get-tuple-element.173.refs_0_), channel_id=1, source_target_pairs={{0,4},{1,5},{2,6},{3,7},{4,0},{5,1},{6,2},{7,3},{8,12},{9,13},{10,... | collective-permute-start | bytes 294920 | tf_op jit(solution)/shard_map/ppermute | solution.py:1354
  190.4 5.0 %collective-permute-start.19 = (bf16[128,384]{1,0:T(8,128)(2,1)S(1)}, bf16[128,384]{1,0:T(8,128)(2,1)}, u32[]{:S(2)}, u32[]{:S(2)}) collective-permute-start(bf16[128,384]{1,0:T(8,128)(2,1)S(1)} %get-tuple-element.174.refs_1_), channel_id=1, source_target_pairs={{0,1},{1,0},{2,3},{3,2},{4,5},{5,4},{6,7},{7,6},{8,9},{9,8},{10,11... | collective-permute-start | bytes 294920 | tf_op jit(solution)/shard_map/ppermute | solution.py:1354
  190.9 4.8 %collective-permute-start.20 = (bf16[128,384]{1,0:T(8,128)(2,1)S(1)}, bf16[128,384]{1,0:T(8,128)(2,1)}, u32[]{:S(2)}, u32[]{:S(2)}) collective-permute-start(bf16[128,384]{1,0:T(8,128)(2,1)S(1)} %get-tuple-element.175.refs_2_), channel_id=1, source_target_pairs={{0,2},{1,3},{2,0},{3,1},{4,6},{5,7},{6,4},{7,5},{8,10},{9,11},{10,... | collective-permute-start | bytes 294920 | tf_op jit(solution)/shard_map/ppermute | solution.py:1354
  196.7 8.2 %collective-permute-start.21 = (bf16[256,384]{1,0:T(8,128)(2,1)S(1)}, bf16[256,384]{1,0:T(8,128)(2,1)S(1)}, u32[]{:S(2)}, u32[]{:S(2)}) collective-permute-start(bf16[256,384]{1,0:T(8,128)(2,1)S(1)} %get-tuple-element.180.refs_0_), channel_id=1, source_target_pairs={{0,2},{1,3},{2,0},{3,1},{4,6},{5,7},{6,4},{7,5},{8,10},{9,11},{10,... | collective-permute-start | bytes 589832 | tf_op jit(solution)/shard_map/ppermute | solution.py:1354
  198.2 6.7 %collective-permute-start.22 = (bf16[256,384]{1,0:T(8,128)(2,1)S(1)}, bf16[256,384]{1,0:T(8,128)(2,1)S(1)}, u32[]{:S(2)}, u32[]{:S(2)}) collective-permute-start(bf16[256,384]{1,0:T(8,128)(2,1)S(1)} %get-tuple-element.181.refs_1_), channel_id=1, source_target_pairs={{0,4},{1,5},{2,6},{3,7},{4,0},{5,1},{6,2},{7,3},{8,12},{9,13},{10,... | collective-permute-start | bytes 589832 | tf_op jit(solution)/shard_map/ppermute | solution.py:1354
  199.5 5.7 %collective-permute-start.23 = (bf16[256,384]{1,0:T(8,128)(2,1)S(1)}, bf16[256,384]{1,0:T(8,128)(2,1)S(1)}, u32[]{:S(2)}, u32[]{:S(2)}) collective-permute-start(bf16[256,384]{1,0:T(8,128)(2,1)S(1)} %get-tuple-element.182.refs_2_), channel_id=1, source_target_pairs={{0,1},{1,0},{2,3},{3,2},{4,5},{5,4},{6,7},{7,6},{8,9},{9,8},{10,11... | collective-permute-start | bytes 589832 | tf_op jit(solution)/shard_map/ppermute | solution.py:1354
  205.9 9.1 %collective-permute-start.25 = (bf16[512,384]{1,0:T(8,128)(2,1)S(1)}, bf16[512,384]{1,0:T(8,128)(2,1)S(1)}, u32[]{:S(2)}, u32[]{:S(2)}) collective-permute-start(bf16[512,384]{1,0:T(8,128)(2,1)S(1)} %get-tuple-element.187.refs_0_), channel_id=1, source_target_pairs={{0,1},{1,0},{2,3},{3,2},{4,5},{5,4},{6,7},{7,6},{8,9},{9,8},{10,11... | collective-permute-start | bytes 1179656 | tf_op jit(solution)/shard_map/ppermute | solution.py:1354
  206.8 9.0 %collective-permute-start.26 = (bf16[512,384]{1,0:T(8,128)(2,1)S(1)}, bf16[512,384]{1,0:T(8,128)(2,1)S(1)}, u32[]{:S(2)}, u32[]{:S(2)}) collective-permute-start(bf16[512,384]{1,0:T(8,128)(2,1)S(1)} %get-tuple-element.188.refs_1_), channel_id=1, source_target_pairs={{0,2},{1,3},{2,0},{3,1},{4,6},{5,7},{6,4},{7,5},{8,10},{9,11},{10,... | collective-permute-start | bytes 1179656 | tf_op jit(solution)/shard_map/ppermute | solution.py:1354
  207.6 8.5 %collective-permute-start.27 = (bf16[512,384]{1,0:T(8,128)(2,1)S(1)}, bf16[512,384]{1,0:T(8,128)(2,1)S(1)}, u32[]{:S(2)}, u32[]{:S(2)}) collective-permute-start(bf16[512,384]{1,0:T(8,128)(2,1)S(1)} %get-tuple-element.189.refs_2_), channel_id=1, source_target_pairs={{0,4},{1,5},{2,6},{3,7},{4,0},{5,1},{6,2},{7,3},{8,12},{9,13},{10,... | collective-permute-start | bytes 1179656 | tf_op jit(solution)/shard_map/ppermute | solution.py:1354
where the time goes:
time: 221 us; the launch traced here: 219 us
  Pallas kernels  107 us (48%)
  starting transfers between devices  49.4 us (22%)
  waiting for transfers between devices  46.4 us (21%)
  other arithmetic  8.65 us (4%)
  local copies, waits for them, and re-layouts  4.86 us (2%)
    all_to_all x4, starting transfers between devices, exchange(): lax.all_to_all(rows.reshape(senders, capacity, half), 'seq', split_axis=0...  25.5 us
    ppermute x19, starting transfers between devices, trade(): return lax.ppermute(rows, 'seq', [(i, i ^ 1 << bit) for i in range(count)])  23 us
    all_to_all x4, waiting for transfers between devices, exchange(): lax.all_to_all(rows.reshape(senders, capacity, half), 'seq', split_axis=0...  22.7 us
    pallas_call x1, Pallas kernels, back_pass(): pl.pallas_call(back_kernel, out_shape=[hbm_out((tok_count, width), jnp.fl...  20.7 us
    pallas_call x1, Pallas kernels, expert(): pl.pallas_call(expert_kernel, grid=(slots // tile,), out_shape=[hbm_out((...  14.7 us
    pallas_call x1, Pallas kernels, expert_grads(): pl.pallas_call(expert_grads_kernel, grid=(units // tile,), out_shape=[hbm...  13.7 us
    ppermute x9, waiting for transfers between devices, swap_heads(): return lax.ppermute(rows, 'heads', [(0, 1), (1, 0)])  12.7 us
    pallas_call x1, Pallas kernels, attend(): pl.pallas_call(partial(attend_kernel, block_rows), out_shape=[jax.ShapeDt...  11.8 us
  transfers between devices with their start and end apart: 32, of which 21 were waited for; matrix products, arithmetic and copies ran while one was open for 4% of the time, Pallas kernels for 38%

commit v1 on v0

--- a/solution.py
+++ b/solution.py
@@ -900,7 +900,7 @@
 def normed_back(grads, w_query, w_key, w_value):
     tok_count = grads.shape[0]
     width, own = w_query.shape
-    tile = 256
+    tile = 512
     whole = pl.BlockSpec((width, own), lambda step: (0, 0))
     return pl.pallas_call(
         normed_back_kernel,

time: 221 us -> 220 us (level)
  no operation moved by 1% of the time
where the time goes in v1:
time: 220 us; the launch traced here: 219 us
  Pallas kernels  107 us (49%)
  starting transfers between devices  48.4 us (22%)
  waiting for transfers between devices  47.6 us (22%)
  other arithmetic  8.65 us (4%)
  local copies, waits for them, and re-layouts  4.86 us (2%)
    all_to_all x4, starting transfers between devices, exchange(): lax.all_to_all(rows.reshape(senders, capacity, half), 'seq', split_axis=0...  25.5 us
    all_to_all x4, waiting for transfers between devices, exchange(): lax.all_to_all(rows.reshape(senders, capacity, half), 'seq', split_axis=0...  22.7 us
    ppermute x19, starting transfers between devices, trade(): return lax.ppermute(rows, 'seq', [(i, i ^ 1 << bit) for i in range(count)])  22 us
    pallas_call x1, Pallas kernels, back_pass(): pl.pallas_call(back_kernel, out_shape=[hbm_out((tok_count, width), jnp.fl...  20.7 us
    pallas_call x1, Pallas kernels, expert(): pl.pallas_call(expert_kernel, grid=(slots // tile,), out_shape=[hbm_out((...  14.7 us
    pallas_call x1, Pallas kernels, expert_grads(): pl.pallas_call(expert_grads_kernel, grid=(units // tile,), out_shape=[hbm...  13.7 us
    ppermute x9, waiting for transfers between devices, swap_heads(): return lax.ppermute(rows, 'heads', [(0, 1), (1, 0)])  12.7 us
    ppermute x19, waiting for transfers between devices, trade(): return lax.ppermute(rows, 'seq', [(i, i ^ 1 << bit) for i in range(count)])  12.2 us
  transfers between devices with their start and end apart: 32, of which 21 were waited for; matrix products, arithmetic and copies ran while one was open for 4% of the time, Pallas kernels for 38%

profile of v1, /device:TPU:0, one launch (start us, length us, event | category | flops | bytes accessed | tf_op | source)
XLA Modules:
  0.0 218.9 jit_solution(12869146971324993328)
XLA Ops:
  0.7 4.3 %route.1 = (s32[1,1024]{1,0:T(1,128)}, bf16[1280,384]{1,0:T(8,128)(2,1)}) custom-call(s32[2]{0:T(128)S(1)} %pad_add_fusion.1.where_ref, s32[1,1024]{1,0:T(1,128)} %bitcast.34, bf16[1024,768]{1,0:T(8,128)(2,1)} %grad_hbm.3), custom_call_target="tpu_custom_call" | custom-call | flops 1006632960 | bytes 4000000 | tf_op jit(solution)/shard_map/route/pallas_call | solution.py:475
  5.0 8.3 %all-to-all-start = ((bf16[16,80,384]{2,1,0:T(8,128)(2,1)}), bf16[16,80,384]{2,1,0:T(8,128)(2,1)S(1)}, u32[]{:S(2)}, u32[]{:S(2)}) async-start(bf16[16,80,384]{2,1,0:T(8,128)(2,1)} %bitcast.7), calls=%async_computation | async-start | bytes 1966080 | tf_op jit(solution)/shard_map/all_to_all | solution.py:1395
  13.4 11.8 %attend.1 = (bf16[1024,768]{1,0:T(8,128)(2,1)S(1)}, bf16[1024,768]{1,0:T(8,128)(2,1)}, bf16[1024,384]{1,0:T(8,128)(2,1)}, bf16[1024,384]{1,0:T(8,128)(2,1)}, bf1...) custom-call(s32[5]{0:T(128)S(1)} %copy-done.10, ...), custom_call_target="tpu_custom_call" | custom-call | flops 2919235584 | bytes 16000000 | tf_op jit(solution)/shard_map/attend/pallas_call | solution.py:289
  25.4 3.4 %collective-permute-done.other_ref = bf16[1024,768]{1,0:T(8,128)(2,1)S(1)} collective-permute-done((bf16[1024,768]{1,0:T(8,128)(2,1)S(1)}, bf16[1024,768]{1,0:T(8,128)(2,1)S(1)}, u32[]{:S(2)}, u32[]{:S(2)}) %collective-permute-start) | collective-permute-done | bytes 1572896 | tf_op jit(solution)/shard_map/ppermute | solution.py:1349
  28.7 5.4 %second.1 = (f32[1024,768]{1,0:T(8,128)}, bf16[1280,384]{1,0:T(8,128)(2,1)}) custom-call(s32[2]{0:T(128)S(1)} %pad_add_fusion.1.where_ref, bf16[1024,768]{1,0:T(8,128)(2,1)} %tokens_ref, bf16[1024,768]{1,0:T(8,128)(2,1)S(1)} %get-tuple-element.111.own_ref, bf16[1024,768]{1,0:T(8,128)(2,1)S(1)} %collective-permute-done.other_ref, ...), custom_call_target="tpu_custom_call" | custom-call | flops 1006632960 | bytes 13000000 | tf_op jit(solution)/shard_map/second/pallas_call | solution.py:536
  34.1 2.4 %all-to-all-done = bf16[16,80,384]{2,1,0:T(8,128)(2,1)S(1)} async-done(((bf16[16,80,384]{2,1,0:T(8,128)(2,1)}), bf16[16,80,384]{2,1,0:T(8,128)(2,1)S(1)}, u32[]{:S(2)}, u32[]{:S(2)}) %all-to-all-start) | async-done | bytes 983072 | tf_op jit(solution)/shard_map/all_to_all | solution.py:1395
  36.6 5.7 %all-to-all-start.1 = ((bf16[16,80,384]{2,1,0:T(8,128)(2,1)}), bf16[16,80,384]{2,1,0:T(8,128)(2,1)S(1)}, u32[]{:S(2)}, u32[]{:S(2)}) async-start(bf16[16,80,384]{2,1,0:T(8,128)(2,1)} %bitcast.9), calls=%async_computation.1 | async-start | bytes 1966080 | tf_op jit(solution)/shard_map/all_to_all | solution.py:1395
  42.3 2.6 %collective-permute-done.1.other_ref.grad_other_hbm = bf16[1280,384]{1,0:T(8,128)(2,1)S(1)} collective-permute-done((bf16[1280,384]{1,0:T(8,128)(2,1)S(1)}, bf16[1280,384]{1,0:T(8,128)(2,1)S(1)}, u32[]{:S(2)}, u32[]{:S(2)}) %collective-permute-start.1) | collective-permute-done | bytes 983072 | tf_op jit(solution)/shard_map/ppermute | solution.py:1349
  44.9 2.0 copy-done.6
  46.9 5.6 %hidden_grad.1.hg_ref = bf16[1280,1536]{1,0:T(8,128)(2,1)} custom-call(s32[2]{0:T(128)S(1)} %pad_add_fusion.1.where_ref, bf16[1280,384]{1,0:T(8,128)(2,1)S(1)} %bitcast.22, bf16[1280,384]{1,0:T(8,128)(2,1)S(1)} %collective-permute-done.1.other_ref.grad_other_hbm, bf16[1536,768]{1,0:T(8,128)(2,1)S(1)} %bitcast.28), custom_call_target="tpu_custom_call" | custom-call | flops 3019898880 | bytes 12000000 | tf_op jit(solution)/shard_map/hidden_grad/pallas_call | solution.py:573
  52.6 12.0 %all-to-all-done.1 = bf16[16,80,384]{2,1,0:T(8,128)(2,1)S(1)} async-done(((bf16[16,80,384]{2,1,0:T(8,128)(2,1)}), bf16[16,80,384]{2,1,0:T(8,128)(2,1)S(1)}, u32[]{:S(2)}, u32[]{:S(2)}) %all-to-all-start.1) | async-done | bytes 983072 | tf_op jit(solution)/shard_map/all_to_all | solution.py:1395
  64.7 2.4 %collective-permute-done.2.other_ref.other_hbm = bf16[1280,384]{1,0:T(8,128)(2,1)S(1)} collective-permute-done((bf16[1280,384]{1,0:T(8,128)(2,1)S(1)}, bf16[1280,384]{1,0:T(8,128)(2,1)S(1)}, u32[]{:S(2)}, u32[]{:S(2)}) %collective-permute-start.2) | collective-permute-done | bytes 983072 | tf_op jit(solution)/shard_map/ppermute | solution.py:1349
  67.1 14.7 %expert.1 = (bf16[1280,1536]{1,0:T(8,128)(2,1)}, bf16[1280,1536]{1,0:T(8,128)(2,1)}, f32[1280,384]{1,0:T(8,128)S(1)}, bf16[1280,384]{1,0:T(8,128)(2,1)S(1)}, bf16[1280,16]{1,0:T(8,128)(2,1)}) custom-call(s32[2]{0:T(128)S(1)} %pad_add_fusion.1.where_ref, bf16[1280,384]{1,0:T(8,128)(2,1)S(1)} %bitcast.25, ...), custom_call_target="tpu_custom_call" | custom-call | flops 6039797760 | bytes 20000000 | tf_op jit(solution)/shard_map/expert/pallas_call | solution.py:650
  82.1 2.4 %collective-permute-done.3 = bf16[1280,384]{1,0:T(8,128)(2,1)S(1)} collective-permute-done((bf16[1280,384]{1,0:T(8,128)(2,1)S(1)}, bf16[1280,384]{1,0:T(8,128)(2,1)S(1)}, u32[]{:S(2)}, u32[]{:S(2)}) %collective-permute-start.3) | collective-permute-done | bytes 983072 | tf_op jit(solution)/shard_map/ppermute | solution.py:1349
  84.5 1.2 add_convert_fusion.1
  85.7 5.7 %all-to-all-start.2 = ((bf16[16,80,384]{2,1,0:T(8,128)(2,1)}), bf16[16,80,384]{2,1,0:T(8,128)(2,1)}, u32[]{:S(2)}, u32[]{:S(2)}) async-start(bf16[16,80,384]{2,1,0:T(8,128)(2,1)} %bitcast.13), calls=%async_computation.2 | async-start | bytes 1966080 | tf_op jit(solution)/shard_map/all_to_all | solution.py:1395
  91.5 1.7 copy-done.7
  93.1 8.0 %expert_out.1 = (f32[1280,384]{1,0:T(8,128)S(1)}, bf16[1280,384]{1,0:T(8,128)(2,1)S(1)}, f32[16,768]{1,0:T(8,128)}, s32[1024,128]{1,0:T(8,128)}) custom-call(s32[2]{0:T(128)S(1)} %pad_add_fusion.1.where_ref, bf16[1280,1536]{1,0:T(8,128)(2,1)} %get-tuple-element.122.hidden_ref, bf16[1280,384]{1,0:T(8,128)(2,1)} %bitcast.26, bf16[1280,384]{1,0:T(8,128)(2,1)} %copy-done.9, ...), custom_call_target="tpu_custom_call" | custom-call | flops 3019898880 | bytes 9000000 | tf_op jit(solution)/shard_map/expert_out/pallas_call | solution.py:717
  101.6 2.0 collective-permute-done.5
  104.3 2.3 %add_convert_fusion = bf16[1280,384]{1,0:T(8,128)(2,1)} fusion(f32[1280,384]{1,0:T(8,128)S(1)} %get-tuple-element.126, bf16[1280,384]{1,0:T(8,128)(2,1)} %collective-permute-done.4), kind=kLoop, calls=%fused_computation | loop fusion | flops 1474560 | bytes 3932160 | tf_op jit(solution)/shard_map/convert_element_type | solution.py:1400
  106.7 8.3 %all-to-all-done.2 = bf16[16,80,384]{2,1,0:T(8,128)(2,1)} async-done(((bf16[16,80,384]{2,1,0:T(8,128)(2,1)}), bf16[16,80,384]{2,1,0:T(8,128)(2,1)}, u32[]{:S(2)}, u32[]{:S(2)}) %all-to-all-start.2) | async-done | bytes 983072 | tf_op jit(solution)/shard_map/all_to_all | solution.py:1395
  115.0 5.8 %all-to-all-start.3 = ((bf16[16,80,384]{2,1,0:T(8,128)(2,1)}), bf16[16,80,384]{2,1,0:T(8,128)(2,1)S(1)}, u32[]{:S(2)}, u32[]{:S(2)}) async-start(bf16[16,80,384]{2,1,0:T(8,128)(2,1)} %bitcast.31), calls=%async_computation.3 | async-start | bytes 1966080 | tf_op jit(solution)/shard_map/all_to_all | solution.py:1395
  120.8 20.7 %back.1 = (f32[1024,768]{1,0:T(8,128)}, bf16[1024,1152]{1,0:T(8,128)(2,1)}, bf16[544,384]{1,0:T(8,128)(2,1)}, bf16[512,384]{1,0:T(8,128)(2,1)}, bf16[512,384]{1,...) custom-call(s32[3]{0:T(128)S(1)} %pad_add_fusion.bits_ref, ...), custom_call_target="tpu_custom_call" | custom-call | flops 6291456000 | bytes 25000000 | tf_op jit(solution)/shard_map/back/pallas_call | solution.py:1163
  141.6 2.0 collective-permute-start.7
  143.6 1.5 collective-permute-start.8
  145.0 1.4 collective-permute-start.9
  146.6 0.9 copy-done.11
  147.5 6.2 %output.1 = bf16[1024,384]{1,0:T(8,128)(2,1)} custom-call(s32[2]{0:T(128)S(1)} %pad_add_fusion.1.where_ref, s32[1024,128]{1,0:T(8,128)} %get-tuple-element.124.col_hbm.col_ref, bf16[1280,384]{1,0:T(8,128)(2,1)} %bitcast.30, f32[1024,768]{1,0:T(8,128)} %get-tuple-element.130.residual_hbm.residual_ref, f32[1,768]{1,0:T(1,128)S(1)} %reshape.103.gain_ref.gain_two_ref, ...), custom_call_target="tpu_custom_call" | custom-call | flops 1006632960 | bytes 6000000 | tf_op jit(solution)/shard_map/output/pallas_call | solution.py:868
  154.5 1.2 collective-permute-done.9.refs_5_
  157.2 1.5 collective-permute-start.11
  159.4 4.6 %normed_back.1.own_ref = bf16[1024,768]{1,0:T(8,128)(2,1)S(1)} custom-call(bf16[1024,1152]{1,0:T(8,128)(2,1)} %get-tuple-element.157.grads_ref, bf16[768,384]{1,0:T(8,128)(2,1)} %wq_ref.1, bf16[768,384]{1,0:T(8,128)(2,1)} %wk_ref.1, bf16[768,384]{1,0:T(8,128)(2,1)} %wv_ref.1), custom_call_target="tpu_custom_call" | custom-call | flops 1811939328 | bytes 6000000 | tf_op jit(solution)/shard_map/normed_back/pallas_call | solution.py:905
  166.8 1.5 collective-permute-start.15
  168.2 2.8 %collective-permute-done.14.refs_4_ = bf16[128,384]{1,0:T(8,128)(2,1)S(1)} collective-permute-done((bf16[128,384]{1,0:T(8,128)(2,1)S(1)}, bf16[128,384]{1,0:T(8,128)(2,1)S(1)}, u32[]{:S(2)}, u32[]{:S(2)}) %collective-permute-start.14) | collective-permute-done | bytes 98336 | tf_op jit(solution)/shard_map/ppermute | solution.py:1354
  171.6 2.4 %collective-permute-start.17 = (bf16[416,384]{1,0:T(8,128)(2,1)S(1)}, bf16[416,384]{1,0:T(8,128)(2,1)S(1)}, u32[]{:S(2)}, u32[]{:S(2)}) collective-permute-start(bf16[416,384]{1,0:T(8,128)(2,1)S(1)} %pack.1.own_ref), channel_id=1, source_target_pairs={{0,8},{1,9},{2,10},{3,11},{4,12},{5,13},{6,14},{7,15},{8,0},{9,1},... | collective-permute-start | bytes 958472 | tf_op jit(solution)/shard_map/ppermute | solution.py:1354
  174.0 13.7 %expert_grads.1 = (f32[768,1536]{1,0:T(8,128)}, f32[1536,768]{1,0:T(8,128)}) custom-call(s32[2]{0:T(128)S(1)} %pad_add_fusion.1.where_ref, bf16[1280,384]{1,0:T(8,128)(2,1)} %bitcast.27, bf16[1280,384]{1,0:T(8,128)(2,1)} %copy-done.9, bf16[1280,384]{1,0:T(8,128)(2,1)} %bitcast.23, bf16[1280,384]{1,0:T(8,128)(2,1)} %copy-done.8, ...), custom_call_target="tpu_custom_call" | custom-call | flops 6039797760 | bytes 22000000 | tf_op jit(solution)/shard_map/expert_grads/pallas_call | solution.py:799
  189.9 1.0 collective-permute-start.19
  190.8 1.5 collective-permute-start.20
  192.9 1.5 collective-permute-done.18.refs_3_
  195.6 1.0 join.2
  196.6 1.5 collective-permute-start.21
  199.0 1.0 collective-permute-start.23
  201.4 1.4 slice_reduce_fusion
  202.8 1.7 fusion
  205.4 1.1 collective-permute-start.25
  206.4 1.1 collective-permute-start.26
  208.2 5.2 %input_back.1 = f32[1024,768]{1,0:T(8,128)} custom-call(bf16[1024,768]{1,0:T(8,128)(2,1)} %tokens_ref, bf16[1024,768]{1,0:T(8,128)(2,1)S(1)} %normed_back.1.own_ref, bf16[1024,768]{1,0:T(8,128)(2,1)S(1)} %collective-permute-done.16.other_ref, f32[1,768]{1,0:T(1,128)S(1)} %reshape.102.gain_ref.gain_one_ref, f32[1024,768]{1,0:T(8,128)} %get-tuple-element.191.residual_ref), custom_call_target="tpu_custom_call" | custom-call | flops 7864320 | bytes 11000000 | tf_op jit(solution)/shard_map/input_back/pallas_call | solution.py:934
  213.3 1.2 collective-permute-done.25.refs_3_
  215.9 2.8 %finish.1 = (f32[768,384]{1,0:T(8,128)}, f32[768,384]{1,0:T(8,128)}, f32[768,384]{1,0:T(8,128)}, f32[384,768]{1,0:T(8,128)}) custom-call(s32[3]{0:T(128)S(1)} %pad_add_fusion.bits_ref, bf16[512,384]{1,0:T(8,128)(2,1)S(1)} %get-tuple-element.187.refs_0_, bf16[512,384]{1,0:T(8,128)(2,1)S(1)} %get-tuple-element.188.refs_1_, ...), custom_call_target="tpu_custom_call" | custom-call | tf_op jit(solution)/shard_map/finish/pallas_call | solution.py:1336
  (84 shorter events, 17.2 us)
Async XLA Ops:
  0.7 12.7 %copy-start.13 = (bf16[768]{0:T(1024)(128)(2,1)S(1)}, bf16[768]{0:T(1024)(128)(2,1)}, u32[]{:S(2)}) copy-start(bf16[768]{0:T(1024)(128)(2,1)} %param.15) | copy-start | bytes 4612
  0.7 12.7 %copy-start.14 = (bf16[32,6]{0,1:T(8,128)(2,1)S(1)}, bf16[32,6]{0,1:T(8,128)(2,1)}, u32[]{:S(2)}) copy-start(bf16[32,6]{0,1:T(8,128)(2,1)} %param.20) | copy-start | bytes 1156
  0.7 12.7 %copy-start.10 = (s32[5]{0:T(128)S(1)}, s32[5]{0:T(128)}, u32[]{:S(2)}) copy-start(s32[5]{0:T(128)} %lengths_ref.1) | copy-start | bytes 64
  5.0 31.5 %all-to-all-start = ((bf16[16,80,384]{2,1,0:T(8,128)(2,1)}), bf16[16,80,384]{2,1,0:T(8,128)(2,1)S(1)}, u32[]{:S(2)}, u32[]{:S(2)}) async-start(bf16[16,80,384]{2,1,0:T(8,128)(2,1)} %bitcast.7), calls=%async_computation | async-start | bytes 1966080 | tf_op jit(solution)/shard_map/all_to_all | solution.py:1395
  13.4 11.9 %copy-start.15 = (bf16[768]{0:T(1024)(128)(2,1)S(1)}, bf16[768]{0:T(1024)(128)(2,1)}, u32[]{:S(2)}) copy-start(bf16[768]{0:T(1024)(128)(2,1)} %param.21) | copy-start | bytes 4612
  25.3 3.5 %collective-permute-start = (bf16[1024,768]{1,0:T(8,128)(2,1)S(1)}, bf16[1024,768]{1,0:T(8,128)(2,1)S(1)}, u32[]{:S(2)}, u32[]{:S(2)}) collective-permute-start(bf16[1024,768]{1,0:T(8,128)(2,1)S(1)} %get-tuple-element.111.own_ref), channel_id=1, source_target_pairs={{0,16},{16,0},{1,17},{17,1},{2,18},{18,2},{3,19},{19,3},{4,20},{20... | collective-permute-start | bytes 4718600 | tf_op jit(solution)/shard_map/ppermute | solution.py:1349
  36.6 16.0 %copy-start = (bf16[16,80,384]{2,1,0:T(8,128)(2,1)}, bf16[16,80,384]{2,1,0:T(8,128)(2,1)S(1)}, u32[]{:S(2)}) copy-start(bf16[16,80,384]{2,1,0:T(8,128)(2,1)S(1)} %all-to-all-done) | copy-start | bytes 2949124
  36.6 28.0 %all-to-all-start.1 = ((bf16[16,80,384]{2,1,0:T(8,128)(2,1)}), bf16[16,80,384]{2,1,0:T(8,128)(2,1)S(1)}, u32[]{:S(2)}, u32[]{:S(2)}) async-start(bf16[16,80,384]{2,1,0:T(8,128)(2,1)} %bitcast.9), calls=%async_computation.1 | async-start | bytes 1966080 | tf_op jit(solution)/shard_map/all_to_all | solution.py:1395
  42.3 2.6 %collective-permute-start.1 = (bf16[1280,384]{1,0:T(8,128)(2,1)S(1)}, bf16[1280,384]{1,0:T(8,128)(2,1)S(1)}, u32[]{:S(2)}, u32[]{:S(2)}) collective-permute-start(bf16[1280,384]{1,0:T(8,128)(2,1)S(1)} %bitcast.21), channel_id=1, source_target_pairs={{0,16},{16,0},{1,17},{17,1},{2,18},{18,2},{3,19},{19,3},{4,20},{20... | collective-permute-start | bytes 2949128 | tf_op jit(solution)/shard_map/ppermute | solution.py:1349
  44.9 7.7 %copy-start.8 = (bf16[1280,384]{1,0:T(8,128)(2,1)}, bf16[1280,384]{1,0:T(8,128)(2,1)S(1)}, u32[]{:S(2)}) copy-start(bf16[1280,384]{1,0:T(8,128)(2,1)S(1)} %collective-permute-done.1.other_ref.grad_other_hbm) | copy-start | bytes 2949124
  44.9 2.0 copy-start.6
  46.9 17.7 %copy-start.12 = (bf16[768,16]{0,1:T(8,128)(2,1)S(1)}, bf16[768,16]{0,1:T(8,128)(2,1)}, u32[]{:S(2)}) copy-start(bf16[768,16]{0,1:T(8,128)(2,1)} %param.22) | copy-start | bytes 73732
  64.6 17.3 %copy-start.1 = (bf16[16,80,384]{2,1,0:T(8,128)(2,1)}, bf16[16,80,384]{2,1,0:T(8,128)(2,1)S(1)}, u32[]{:S(2)}) copy-start(bf16[16,80,384]{2,1,0:T(8,128)(2,1)S(1)} %all-to-all-done.1) | copy-start | bytes 2949124
  64.6 2.6 %collective-permute-start.2 = (bf16[1280,384]{1,0:T(8,128)(2,1)S(1)}, bf16[1280,384]{1,0:T(8,128)(2,1)S(1)}, u32[]{:S(2)}, u32[]{:S(2)}) collective-permute-start(bf16[1280,384]{1,0:T(8,128)(2,1)S(1)} %bitcast.24), channel_id=1, source_target_pairs={{0,16},{16,0},{1,17},{17,1},{2,18},{18,2},{3,19},{19,3},{4,20},{20... | collective-permute-start | bytes 2949128 | tf_op jit(solution)/shard_map/ppermute | solution.py:1349
  67.1 14.7 %copy-start.9 = (bf16[1280,384]{1,0:T(8,128)(2,1)}, bf16[1280,384]{1,0:T(8,128)(2,1)S(1)}, u32[]{:S(2)}) copy-start(bf16[1280,384]{1,0:T(8,128)(2,1)S(1)} %collective-permute-done.2.other_ref.other_hbm) | copy-start | bytes 2949124
  81.9 2.6 %collective-permute-start.3 = (bf16[1280,384]{1,0:T(8,128)(2,1)S(1)}, bf16[1280,384]{1,0:T(8,128)(2,1)S(1)}, u32[]{:S(2)}, u32[]{:S(2)}) collective-permute-start(bf16[1280,384]{1,0:T(8,128)(2,1)S(1)} %get-tuple-element.120), channel_id=1, source_target_pairs={{0,16},{16,0},{1,17},{17,1},{2,18},{18,2},{3,19},{19,3},{4,20},{20... | collective-permute-start | bytes 2949128 | tf_op jit(solution)/shard_map/ppermute | solution.py:1349
  85.7 29.2 %all-to-all-start.2 = ((bf16[16,80,384]{2,1,0:T(8,128)(2,1)}), bf16[16,80,384]{2,1,0:T(8,128)(2,1)}, u32[]{:S(2)}, u32[]{:S(2)}) async-start(bf16[16,80,384]{2,1,0:T(8,128)(2,1)} %bitcast.13), calls=%async_computation.2 | async-start | bytes 1966080 | tf_op jit(solution)/shard_map/all_to_all | solution.py:1395
  91.5 1.7 copy-start.7
  101.1 3.2 %collective-permute-start.4 = (bf16[1280,384]{1,0:T(8,128)(2,1)S(1)}, bf16[1280,384]{1,0:T(8,128)(2,1)}, u32[]{:S(2)}, u32[]{:S(2)}) collective-permute-start(bf16[1280,384]{1,0:T(8,128)(2,1)S(1)} %get-tuple-element.127), channel_id=1, source_target_pairs={{0,16},{16,0},{1,17},{17,1},{2,18},{18,2},{3,19},{19,3},{4,20},{20... | collective-permute-start | bytes 2949128 | tf_op jit(solution)/shard_map/ppermute | solution.py:1349
  101.1 2.5 %collective-permute-start.5 = (f32[16,768]{1,0:T(8,128)}, f32[16,768]{1,0:T(8,128)S(1)}, u32[]{:S(2)}, u32[]{:S(2)}) collective-permute-start(f32[16,768]{1,0:T(8,128)} %get-tuple-element.128), channel_id=1, source_target_pairs={{0,16},{16,0},{1,17},{17,1},{2,18},{18,2},{3,19},{19,3},{4,20},{20... | collective-permute-start | bytes 147464 | tf_op jit(solution)/shard_map/ppermute | solution.py:1349
  114.9 5.9 %collective-permute-start.6 = (bf16[1280,384]{1,0:T(8,128)(2,1)}, bf16[1280,384]{1,0:T(8,128)(2,1)S(1)}, u32[]{:S(2)}, u32[]{:S(2)}) collective-permute-start(bf16[1280,384]{1,0:T(8,128)(2,1)} %bitcast.14.own_hbm), channel_id=1, source_target_pairs={{0,16},{16,0},{1,17},{17,1},{2,18},{18,2},{3,19},{19,3},{4,20},{20... | collective-permute-start | bytes 2949128 | tf_op jit(solution)/shard_map/ppermute | solution.py:1349
  115.0 31.6 %all-to-all-start.3 = ((bf16[16,80,384]{2,1,0:T(8,128)(2,1)}), bf16[16,80,384]{2,1,0:T(8,128)(2,1)S(1)}, u32[]{:S(2)}, u32[]{:S(2)}) async-start(bf16[16,80,384]{2,1,0:T(8,128)(2,1)} %bitcast.31), calls=%async_computation.3 | async-start | bytes 1966080 | tf_op jit(solution)/shard_map/all_to_all | solution.py:1395
  141.6 14.1 %collective-permute-start.7 = (bf16[544,384]{1,0:T(8,128)(2,1)}, bf16[544,384]{1,0:T(8,128)(2,1)S(1)}, u32[]{:S(2)}, u32[]{:S(2)}) collective-permute-start(bf16[544,384]{1,0:T(8,128)(2,1)} %get-tuple-element.139.refs_6_), channel_id=1, source_target_pairs={{0,1},{1,0},{2,3},{3,2},{4,5},{5,4},{6,7},{7,6},{8,9},{9,8},{10,11... | collective-permute-start | bytes 1253384 | tf_op jit(solution)/shard_map/ppermute | solution.py:1354
  143.6 10.9 %collective-permute-start.8 = (bf16[512,384]{1,0:T(8,128)(2,1)}, bf16[512,384]{1,0:T(8,128)(2,1)S(1)}, u32[]{:S(2)}, u32[]{:S(2)}) collective-permute-start(bf16[512,384]{1,0:T(8,128)(2,1)} %get-tuple-element.140), channel_id=1, source_target_pairs={{0,2},{1,3},{2,0},{3,1},{4,6},{5,7},{6,4},{7,5},{8,10},{9,11},{10,... | collective-permute-start | bytes 1179656 | tf_op jit(solution)/shard_map/ppermute | solution.py:1354
  145.0 10.6 %collective-permute-start.9 = (bf16[512,384]{1,0:T(8,128)(2,1)}, bf16[512,384]{1,0:T(8,128)(2,1)S(1)}, u32[]{:S(2)}, u32[]{:S(2)}) collective-permute-start(bf16[512,384]{1,0:T(8,128)(2,1)} %get-tuple-element.141), channel_id=1, source_target_pairs={{0,4},{1,5},{2,6},{3,7},{4,0},{5,1},{6,2},{7,3},{8,12},{9,13},{10,... | collective-permute-start | bytes 1179656 | tf_op jit(solution)/shard_map/ppermute | solution.py:1354
  146.6 0.9 copy-start.11
  147.5 8.1 %copy-start.2 = (bf16[544,384]{1,0:T(8,128)(2,1)S(1)}, bf16[544,384]{1,0:T(8,128)(2,1)}, u32[]{:S(2)}) copy-start(bf16[544,384]{1,0:T(8,128)(2,1)} %get-tuple-element.139.refs_6_) | copy-start | bytes 1253380
  147.5 8.1 %copy-start.3 = (bf16[512,384]{1,0:T(8,128)(2,1)S(1)}, bf16[512,384]{1,0:T(8,128)(2,1)}, u32[]{:S(2)}) copy-start(bf16[512,384]{1,0:T(8,128)(2,1)} %get-tuple-element.145.refs_0_) | copy-start | bytes 1179652
  147.5 8.2 %copy-start.4 = (bf16[512,384]{1,0:T(8,128)(2,1)S(1)}, bf16[512,384]{1,0:T(8,128)(2,1)}, u32[]{:S(2)}) copy-start(bf16[512,384]{1,0:T(8,128)(2,1)} %get-tuple-element.146.refs_1_) | copy-start | bytes 1179652
  147.5 8.2 %copy-start.5 = (bf16[512,384]{1,0:T(8,128)(2,1)S(1)}, bf16[512,384]{1,0:T(8,128)(2,1)}, u32[]{:S(2)}) copy-start(bf16[512,384]{1,0:T(8,128)(2,1)} %get-tuple-element.147.refs_2_) | copy-start | bytes 1179652
  156.5 8.3 %collective-permute-start.10 = (bf16[288,384]{1,0:T(8,128)(2,1)S(1)}, bf16[288,384]{1,0:T(8,128)(2,1)S(1)}, u32[]{:S(2)}, u32[]{:S(2)}) collective-permute-start(bf16[288,384]{1,0:T(8,128)(2,1)S(1)} %get-tuple-element.154.refs_6_), channel_id=1, source_target_pairs={{0,2},{1,3},{2,0},{3,1},{4,6},{5,7},{6,4},{7,5},{8,10},{9,11},{10,... | collective-permute-start | bytes 663560 | tf_op jit(solution)/shard_map/ppermute | solution.py:1354
  157.2 6.9 %collective-permute-start.11 = (bf16[256,384]{1,0:T(8,128)(2,1)S(1)}, bf16[256,384]{1,0:T(8,128)(2,1)S(1)}, u32[]{:S(2)}, u32[]{:S(2)}) collective-permute-start(bf16[256,384]{1,0:T(8,128)(2,1)S(1)} %get-tuple-element.155), channel_id=1, source_target_pairs={{0,4},{1,5},{2,6},{3,7},{4,0},{5,1},{6,2},{7,3},{8,12},{9,13},{10,... | collective-permute-start | bytes 589832 | tf_op jit(solution)/shard_map/ppermute | solution.py:1354
  158.6 6.2 %collective-permute-start.12 = (bf16[256,384]{1,0:T(8,128)(2,1)S(1)}, bf16[256,384]{1,0:T(8,128)(2,1)S(1)}, u32[]{:S(2)}, u32[]{:S(2)}) collective-permute-start(bf16[256,384]{1,0:T(8,128)(2,1)S(1)} %get-tuple-element.156), channel_id=1, source_target_pairs={{0,1},{1,0},{2,3},{3,2},{4,5},{5,4},{6,7},{7,6},{8,9},{9,8},{10,11... | collective-permute-start | bytes 589832 | tf_op jit(solution)/shard_map/ppermute | solution.py:1354
  164.9 6.7 %collective-permute-start.16 = (bf16[1024,768]{1,0:T(8,128)(2,1)S(1)}, bf16[1024,768]{1,0:T(8,128)(2,1)S(1)}, u32[]{:S(2)}, u32[]{:S(2)}) collective-permute-start(bf16[1024,768]{1,0:T(8,128)(2,1)S(1)} %normed_back.1.own_ref), channel_id=1, source_target_pairs={{0,16},{16,0},{1,17},{17,1},{2,18},{18,2},{3,19},{19,3},{4,20},{20... | collective-permute-start | bytes 4718600 | tf_op jit(solution)/shard_map/ppermute | solution.py:1349
  165.7 5.8 %collective-permute-start.13 = (bf16[160,384]{1,0:T(8,128)(2,1)S(1)}, bf16[160,384]{1,0:T(8,128)(2,1)S(1)}, u32[]{:S(2)}, u32[]{:S(2)}) collective-permute-start(bf16[160,384]{1,0:T(8,128)(2,1)S(1)} %get-tuple-element.164.refs_6_), channel_id=1, source_target_pairs={{0,4},{1,5},{2,6},{3,7},{4,0},{5,1},{6,2},{7,3},{8,12},{9,13},{10,... | collective-permute-start | bytes 368648 | tf_op jit(solution)/shard_map/ppermute | solution.py:1354
  166.0 5.0 %collective-permute-start.14 = (bf16[128,384]{1,0:T(8,128)(2,1)S(1)}, bf16[128,384]{1,0:T(8,128)(2,1)S(1)}, u32[]{:S(2)}, u32[]{:S(2)}) collective-permute-start(bf16[128,384]{1,0:T(8,128)(2,1)S(1)} %get-tuple-element.165), channel_id=1, source_target_pairs={{0,1},{1,0},{2,3},{3,2},{4,5},{5,4},{6,7},{7,6},{8,9},{9,8},{10,11... | collective-permute-start | bytes 294920 | tf_op jit(solution)/shard_map/ppermute | solution.py:1354
  166.8 4.6 %collective-permute-start.15 = (bf16[128,384]{1,0:T(8,128)(2,1)S(1)}, bf16[128,384]{1,0:T(8,128)(2,1)S(1)}, u32[]{:S(2)}, u32[]{:S(2)}) collective-permute-start(bf16[128,384]{1,0:T(8,128)(2,1)S(1)} %get-tuple-element.166), channel_id=1, source_target_pairs={{0,2},{1,3},{2,0},{3,1},{4,6},{5,7},{6,4},{7,5},{8,10},{9,11},{10,... | collective-permute-start | bytes 294920 | tf_op jit(solution)/shard_map/ppermute | solution.py:1354
  171.6 17.0 %collective-permute-start.17 = (bf16[416,384]{1,0:T(8,128)(2,1)S(1)}, bf16[416,384]{1,0:T(8,128)(2,1)S(1)}, u32[]{:S(2)}, u32[]{:S(2)}) collective-permute-start(bf16[416,384]{1,0:T(8,128)(2,1)S(1)} %pack.1.own_ref), channel_id=1, source_target_pairs={{0,8},{1,9},{2,10},{3,11},{4,12},{5,13},{6,14},{7,15},{8,0},{9,1},... | collective-permute-start | bytes 958472 | tf_op jit(solution)/shard_map/ppermute | solution.py:1354
  189.3 10.8 %collective-permute-start.24 = (f32[16,768]{1,0:T(8,128)}, f32[16,768]{1,0:T(8,128)}, u32[]{:S(2)}, u32[]{:S(2)}) collective-permute-start(f32[16,768]{1,0:T(8,128)} %pad_maximum_fusion), channel_id=1, source_target_pairs={{0,16},{16,0},{1,17},{17,1},{2,18},{18,2},{3,19},{19,3},{4,20},{20... | collective-permute-start | bytes 147464 | tf_op jit(solution)/shard_map/ppermute | solution.py:1349
  189.3 5.2 %collective-permute-start.18 = (bf16[128,384]{1,0:T(8,128)(2,1)S(1)}, bf16[128,384]{1,0:T(8,128)(2,1)S(1)}, u32[]{:S(2)}, u32[]{:S(2)}) collective-permute-start(bf16[128,384]{1,0:T(8,128)(2,1)S(1)} %get-tuple-element.173.refs_0_), channel_id=1, source_target_pairs={{0,4},{1,5},{2,6},{3,7},{4,0},{5,1},{6,2},{7,3},{8,12},{9,13},{10,... | collective-permute-start | bytes 294920 | tf_op jit(solution)/shard_map/ppermute | solution.py:1354
  189.9 5.0 %collective-permute-start.19 = (bf16[128,384]{1,0:T(8,128)(2,1)S(1)}, bf16[128,384]{1,0:T(8,128)(2,1)}, u32[]{:S(2)}, u32[]{:S(2)}) collective-permute-start(bf16[128,384]{1,0:T(8,128)(2,1)S(1)} %get-tuple-element.174.refs_1_), channel_id=1, source_target_pairs={{0,1},{1,0},{2,3},{3,2},{4,5},{5,4},{6,7},{7,6},{8,9},{9,8},{10,11... | collective-permute-start | bytes 294920 | tf_op jit(solution)/shard_map/ppermute | solution.py:1354
  190.8 4.8 %collective-permute-start.20 = (bf16[128,384]{1,0:T(8,128)(2,1)S(1)}, bf16[128,384]{1,0:T(8,128)(2,1)}, u32[]{:S(2)}, u32[]{:S(2)}) collective-permute-start(bf16[128,384]{1,0:T(8,128)(2,1)S(1)} %get-tuple-element.175.refs_2_), channel_id=1, source_target_pairs={{0,2},{1,3},{2,0},{3,1},{4,6},{5,7},{6,4},{7,5},{8,10},{9,11},{10,... | collective-permute-start | bytes 294920 | tf_op jit(solution)/shard_map/ppermute | solution.py:1354
  196.6 7.9 %collective-permute-start.21 = (bf16[256,384]{1,0:T(8,128)(2,1)S(1)}, bf16[256,384]{1,0:T(8,128)(2,1)S(1)}, u32[]{:S(2)}, u32[]{:S(2)}) collective-permute-start(bf16[256,384]{1,0:T(8,128)(2,1)S(1)} %get-tuple-element.180.refs_0_), channel_id=1, source_target_pairs={{0,2},{1,3},{2,0},{3,1},{4,6},{5,7},{6,4},{7,5},{8,10},{9,11},{10,... | collective-permute-start | bytes 589832 | tf_op jit(solution)/shard_map/ppermute | solution.py:1354
  198.1 6.4 %collective-permute-start.22 = (bf16[256,384]{1,0:T(8,128)(2,1)S(1)}, bf16[256,384]{1,0:T(8,128)(2,1)S(1)}, u32[]{:S(2)}, u32[]{:S(2)}) collective-permute-start(bf16[256,384]{1,0:T(8,128)(2,1)S(1)} %get-tuple-element.181.refs_1_), channel_id=1, source_target_pairs={{0,4},{1,5},{2,6},{3,7},{4,0},{5,1},{6,2},{7,3},{8,12},{9,13},{10,... | collective-permute-start | bytes 589832 | tf_op jit(solution)/shard_map/ppermute | solution.py:1354
  199.0 5.7 %collective-permute-start.23 = (bf16[256,384]{1,0:T(8,128)(2,1)S(1)}, bf16[256,384]{1,0:T(8,128)(2,1)S(1)}, u32[]{:S(2)}, u32[]{:S(2)}) collective-permute-start(bf16[256,384]{1,0:T(8,128)(2,1)S(1)} %get-tuple-element.182.refs_2_), channel_id=1, source_target_pairs={{0,1},{1,0},{2,3},{3,2},{4,5},{5,4},{6,7},{7,6},{8,9},{9,8},{10,11... | collective-permute-start | bytes 589832 | tf_op jit(solution)/shard_map/ppermute | solution.py:1354
  205.4 9.2 %collective-permute-start.25 = (bf16[512,384]{1,0:T(8,128)(2,1)S(1)}, bf16[512,384]{1,0:T(8,128)(2,1)S(1)}, u32[]{:S(2)}, u32[]{:S(2)}) collective-permute-start(bf16[512,384]{1,0:T(8,128)(2,1)S(1)} %get-tuple-element.187.refs_0_), channel_id=1, source_target_pairs={{0,1},{1,0},{2,3},{3,2},{4,5},{5,4},{6,7},{7,6},{8,9},{9,8},{10,11... | collective-permute-start | bytes 1179656 | tf_op jit(solution)/shard_map/ppermute | solution.py:1354
  206.4 8.9 %collective-permute-start.26 = (bf16[512,384]{1,0:T(8,128)(2,1)S(1)}, bf16[512,384]{1,0:T(8,128)(2,1)S(1)}, u32[]{:S(2)}, u32[]{:S(2)}) collective-permute-start(bf16[512,384]{1,0:T(8,128)(2,1)S(1)} %get-tuple-element.188.refs_1_), channel_id=1, source_target_pairs={{0,2},{1,3},{2,0},{3,1},{4,6},{5,7},{6,4},{7,5},{8,10},{9,11},{10,... | collective-permute-start | bytes 1179656 | tf_op jit(solution)/shard_map/ppermute | solution.py:1354
  207.6 8.3 %collective-permute-start.27 = (bf16[512,384]{1,0:T(8,128)(2,1)S(1)}, bf16[512,384]{1,0:T(8,128)(2,1)S(1)}, u32[]{:S(2)}, u32[]{:S(2)}) collective-permute-start(bf16[512,384]{1,0:T(8,128)(2,1)S(1)} %get-tuple-element.189.refs_2_), channel_id=1, source_target_pairs={{0,4},{1,5},{2,6},{3,7},{4,0},{5,1},{6,2},{7,3},{8,12},{9,13},{10,... | collective-permute-start | bytes 1179656 | tf_op jit(solution)/shard_map/ppermute | solution.py:1354
